TPU v7x, 256 devices: a whole 4x4x8 slice. The times are simulated.
256 devices in a mesh: rows: 32 (over x_hi, z, core), cols: 8 (over x_lo, y).
Axes of the slice: x: 4 (x_hi: 2, x_lo: 2; x = x_hi * 2 + x_lo), y: 4, z: 8, core: 2. Of those that a mesh axis runs over, the one named last changes fastest.
Arguments:
- object_field: float32 [2, 16384, 4096], P(None, 'rows', 'cols'), may hold values from -6 to 6
- probe: float32 [4, 2, 256, 256], replicated, may hold values from -6 to 6
- photons: int32 [32, 8, 4, 256, 256], P('rows', 'cols'), may hold values from 0 to 40
- positions: int32 [32, 8, 4, 2], P('rows', 'cols'), may hold values from -128 to 384
- live_counts: int32 [32, 8], P('rows', 'cols'), may hold values from 1 to 4, as said below
Outputs:
- object_grad: float32 [2, 16384, 4096], P(None, 'rows', 'cols')
- probe_grad: float32 [4, 2, 256, 256], replicated
Inputs may be any that keep to these rules, and one draw needn't show every extreme that they name: `live_counts`: some tile has 4 live slots in every draw.
All inputs are finite; a program needn't handle non-finite values.
Results may differ from a plain program's by a relative error of at most 0.0039.
The roundings to bfloat16 on the way count: a program that leaves them out, or rounds other values in their place, can miss the bound.
Values sent between devices are 32-bit elements; how exact they have to be, the bound alone decides.
A program may use at most 64 MiB of HBM per device.

v0:
```python
import math

import jax
import jax.numpy as jnp
from jax import lax
from jax.sharding import PartitionSpec as P

background = 1.0


def shifted(value, axis, steps):
    count = lax.axis_size(axis)
    leading, last = (max(0, -steps), min(count, count - steps))
    return lax.ppermute(value, axis, [(source, source + steps) for source in range(leading, last)])


def extended(cells, sides, width):
    for axis, dim in sides:
        count = lax.axis_size(axis)
        ends = count - 1
        head = lax.slice_in_dim(cells, 0, width, axis=dim)
        tail = lax.slice_in_dim(cells, cells.shape[dim] - width, cells.shape[dim], axis=dim)
        cells = jnp.concatenate(
            [
                lax.ppermute(tail, axis, [(i, (i + 1) % count) for i in range(ends)]),
                cells,
                lax.ppermute(head, axis, [((i + 1) % count, i) for i in range(ends)]),
            ],
            axis=dim,
        )
    return cells


def dft_tables(wave_size):
    ramp = jnp.arange(wave_size, dtype=jnp.int32)
    phases = ramp[:, None] * ramp[None, :] % wave_size
    angles = phases.astype(jnp.float32) * (2.0 * math.pi / wave_size)
    scaling = 1.0 / math.sqrt(wave_size)
    return (
        (jnp.cos(angles) * scaling).astype(jnp.bfloat16),
        (jnp.sin(angles) * scaling).astype(jnp.bfloat16),
    )


def batch_left(table, values):
    return jnp.einsum("ab,mbc->mac", table, values, preferred_element_type=jnp.float32)


def batch_right(values, table):
    return jnp.einsum("mab,bc->mac", values, table, preferred_element_type=jnp.float32)


def left_apply(cos_t, sin_t, part_re, part_im, orient):
    out_re = batch_left(cos_t, part_re) - orient * batch_left(sin_t, part_im)
    out_im = batch_left(cos_t, part_im) + orient * batch_left(sin_t, part_re)
    return (out_re, out_im)


def right_apply(cos_t, sin_t, part_re, part_im, orient):
    out_re = batch_right(part_re, cos_t) - orient * batch_right(part_im, sin_t)
    out_im = batch_right(part_im, cos_t) + orient * batch_right(part_re, sin_t)
    return (out_re, out_im)


def slot_terms(patch, counts_here, probe, cos_t, sin_t):
    probe_re, probe_im = (probe[:, 0], probe[:, 1])
    patch_re, patch_im = (patch[0], patch[1])
    exit_re = (probe_re * patch_re - probe_im * patch_im).astype(jnp.bfloat16)
    exit_im = (probe_re * patch_im + probe_im * patch_re).astype(jnp.bfloat16)
    half_re, half_im = left_apply(cos_t, sin_t, exit_re, exit_im, -1.0)
    wave_re, wave_im = right_apply(
        cos_t, sin_t, half_re.astype(jnp.bfloat16), half_im.astype(jnp.bfloat16), -1.0
    )
    intensity = jnp.sum(wave_re * wave_re + wave_im * wave_im, axis=0) + background
    factor = 1.0 - counts_here.astype(jnp.float32) / intensity
    update_re = (factor * wave_re).astype(jnp.bfloat16)
    update_im = (factor * wave_im).astype(jnp.bfloat16)
    back_re, back_im = left_apply(cos_t, sin_t, update_re, update_im, 1.0)
    chi_re, chi_im = right_apply(
        cos_t, sin_t, back_re.astype(jnp.bfloat16), back_im.astype(jnp.bfloat16), 1.0
    )
    object_term = jnp.stack(
        [
            jnp.sum(probe_re * chi_re + probe_im * chi_im, axis=0),
            jnp.sum(probe_re * chi_im - probe_im * chi_re, axis=0),
        ]
    )
    probe_term = jnp.stack(
        [patch_re * chi_re + patch_im * chi_im, patch_re * chi_im - patch_im * chi_re], axis=1
    )
    return (object_term, probe_term)


def pass_rows(rim_cells, offset):
    return shifted(rim_cells, "rows", offset)


def pass_cols(rim_cells, offset):
    return shifted(rim_cells, "cols", offset)


def fold_rims(gradient, rim_width):
    from_below = pass_rows(gradient[:, :rim_width, :], -1)
    from_above = pass_rows(gradient[:, -rim_width:, :], 1)
    middle = gradient[:, rim_width:-rim_width, :]
    middle = middle.at[:, -rim_width:, :].add(from_below)
    middle = middle.at[:, :rim_width, :].add(from_above)
    from_right = pass_cols(middle[:, :, :rim_width], -1)
    from_left = pass_cols(middle[:, :, -rim_width:], 1)
    core = middle[:, :, rim_width:-rim_width]
    core = core.at[:, :, -rim_width:].add(from_right)
    core = core.at[:, :, :rim_width].add(from_left)
    return core


def on_device(object_field, probe, photons, positions, live_counts):
    wave_size = probe.shape[-1]
    rim_width = wave_size // 2
    cos_t, sin_t = dft_tables(wave_size)
    padded = extended(object_field, (("rows", 1), ("cols", 2)), rim_width)
    local_counts = photons[0, 0]
    corners = positions[0, 0] + rim_width
    live_count = live_counts[0, 0]
    slot_total = local_counts.shape[0]
    anchor = jnp.int32(0)

    def visit(slot_id, state):
        gradient, probe_acc = state
        top_row = corners[slot_id, 0]
        left_col = corners[slot_id, 1]
        patch = lax.dynamic_slice(padded, (anchor, top_row, left_col), (2, wave_size, wave_size))
        object_term, probe_term = slot_terms(patch, local_counts[slot_id], probe, cos_t, sin_t)
        alive_flag = slot_id < live_count
        object_term = jnp.where(alive_flag, object_term, 0.0)
        probe_term = jnp.where(alive_flag, probe_term, 0.0)
        before = lax.dynamic_slice(gradient, (anchor, top_row, left_col), (2, wave_size, wave_size))
        gradient = lax.dynamic_update_slice(
            gradient, before + object_term, (anchor, top_row, left_col)
        )
        return (gradient, probe_acc + probe_term)

    start_state = (jnp.zeros(padded.shape, jnp.float32), jnp.zeros(probe.shape, jnp.float32))
    gradient, probe_acc = lax.fori_loop(
        0, slot_total, lambda slot_id, state: visit(slot_id, state), start_state
    )
    object_grad = fold_rims(gradient, rim_width)
    probe_total = lax.psum(probe_acc, ("rows", "cols"))
    probe_grad = probe_total / math.sqrt(lax.axis_size("rows") * lax.axis_size("cols"))
    return (object_grad, probe_grad)


def solution(mesh):
    in_specs = (
        P(None, "rows", "cols"),
        P(),
        P("rows", "cols", None, None, None),
        P("rows", "cols", None, None),
        P("rows", "cols"),
    )
    out_specs = (P(None, "rows", "cols"), P())
    return jax.shard_map(
        on_device, mesh=mesh, in_specs=in_specs, out_specs=out_specs, check_vma=False
    )
```

profile of v0, /device:TPU:1, one launch (start us, length us, event | category | flops | bytes accessed | tf_op | source)
XLA Modules:
  0.0 502.2 jit_solution(7338560956756577695)
XLA Ops:
  8.6 4.9 collective-permute-start
  13.6 1.9 collective-permute-start.1
  15.5 4.2 collective-permute-done
  19.9 4.2 collective-permute-done.1
  27.0 3.2 collective-permute-start.2
  31.6 1.9 copy.23
  33.5 8.2 %collective-permute-done.2 = f32[2,768,128]{2,1,0:T(8,128)S(1)} collective-permute-done((f32[2,768,128]{2,1,0:T(8,128)}, f32[2,768,128]{2,1,0:T(8,128)S(1)}, u32[]{:S(2)}, u32[]{:S(2)}) %collective-permute-start.2) | collective-permute-done | bytes 786464 | tf_op jit(solution)/shard_map/ppermute | solution.py:25
  41.7 4.1 collective-permute-done.3
  45.8 3.7 pad_maximum_fusion
  49.5 2.4 broadcast_in_dim.28
  52.0 157.7 %while.21 = (s32[]{:T(128)}, f32[2,768,768]{2,1,0:T(8,128)}, f32[4,2,256,256]{3,2,0,1:T(8,128)}, s32[4,2]{0,1:T(2,128)S(1)}, s32[]{:T(128)}, /*index=5*/f32[4,2,...) while((s32[]{:T(128)}, f32[2,768,768]{2,1,0:T(8,128)}, ...), condition=%wide.region_4.5_spmd.clone.clone, body=%wide.region_0.4_spmd.clone.clone.sunk | while | flops 2179923968 | bytes 55574800 | solution.py:143
  78.8 1.9 add_bitcast_fusion.3
  82.1 1.7 fusion.248
  83.8 6.3 %dynamic_update_slice.10 = f32[2,768,768]{2,1,0:T(8,128)} dynamic-update-slice(f32[2,768,768]{2,1,0:T(8,128)} %get-tuple-element.466, f32[2,256,256]{2,1,0:T(8,128)S(1)} %fusion.247, s32[]{:T(128)} %constant.170.clone.1..sunk, s32[]{:T(128)S(6)} %select_n.194, s32[]{:T(128)S(6)} %select_n.195) | dynamic-update-slice | bytes 1048580 | tf_op jit(solution)/shard_map/while/body/eval_jaxpr/dynamic_update_slice | solution.py:137
  116.8 1.9 add_bitcast_fusion.3
  120.1 3.3 fusion.248
  123.4 6.5 %dynamic_update_slice.10 = f32[2,768,768]{2,1,0:T(8,128)} dynamic-update-slice(f32[2,768,768]{2,1,0:T(8,128)} %get-tuple-element.466, f32[2,256,256]{2,1,0:T(8,128)S(1)} %fusion.247, s32[]{:T(128)} %constant.170.clone.1..sunk, s32[]{:T(128)S(6)} %select_n.194, s32[]{:T(128)S(6)} %select_n.195) | dynamic-update-slice | bytes 1048580 | tf_op jit(solution)/shard_map/while/body/eval_jaxpr/dynamic_update_slice | solution.py:137
  156.8 1.9 add_bitcast_fusion.3
  160.0 3.3 fusion.248
  163.3 6.5 %dynamic_update_slice.10 = f32[2,768,768]{2,1,0:T(8,128)} dynamic-update-slice(f32[2,768,768]{2,1,0:T(8,128)} %get-tuple-element.466, f32[2,256,256]{2,1,0:T(8,128)S(1)} %fusion.247, s32[]{:T(128)} %constant.170.clone.1..sunk, s32[]{:T(128)S(6)} %select_n.194, s32[]{:T(128)S(6)} %select_n.195) | dynamic-update-slice | bytes 1048580 | tf_op jit(solution)/shard_map/while/body/eval_jaxpr/dynamic_update_slice | solution.py:137
  196.6 1.9 add_bitcast_fusion.3
  199.9 3.3 fusion.248
  203.2 6.5 %dynamic_update_slice.10 = f32[2,768,768]{2,1,0:T(8,128)} dynamic-update-slice(f32[2,768,768]{2,1,0:T(8,128)} %get-tuple-element.466, f32[2,256,256]{2,1,0:T(8,128)S(1)} %fusion.247, s32[]{:T(128)} %constant.170.clone.1..sunk, s32[]{:T(128)S(6)} %select_n.194, s32[]{:T(128)S(6)} %select_n.195) | dynamic-update-slice | bytes 1048580 | tf_op jit(solution)/shard_map/while/body/eval_jaxpr/dynamic_update_slice | solution.py:137
  209.6 2.4 fusion.143
  212.0 1.9 collective-permute-start.4
  213.9 9.1 %collective-permute-start.5 = (f32[2,128,768]{2,1,0:T(8,128)S(1)}, f32[2,128,768]{2,1,0:T(8,128)S(1)}, u32[]{:S(2)}, u32[]{:S(2)}) collective-permute-start(f32[2,128,768]{2,1,0:T(8,128)S(1)} %get-tuple-element.372), channel_id=1, source_target_pairs={{0,8},{8,16},{16,24},{24,32},{32,40},{40,48},{48,56},{56,64},{64,7... | collective-permute-start | bytes 2359304 | tf_op jit(solution)/shard_map/ppermute | solution.py:14
  223.0 3.1 copy.24
  226.1 2.1 slice.160
  228.2 3.1 collective-permute-done.4
  235.4 4.0 collective-permute-start.7
  239.4 250.3 %all-reduce.2.cloned.1.call-done = f32[4,2,256,256]{3,2,1,0:T(8,128)} async-done(((f32[4,2,256,256]{3,2,1,0:T(8,128)}), f32[4,2,256,256]{3,2,1,0:T(8,128)}) %all-reduce.2.cloned.1.call-update) | async-done | bytes 2097168 | tf_op jit(solution)/shard_map/psum | solution.py:147
  489.7 3.1 broadcast_multiply_fusion
  (112 shorter events, 107.2 us)
Async XLA Ops:
  7.2 12.6 %copy-start.3 = (f32[2,512,512]{2,1,0:T(8,128)S(1)}, f32[2,512,512]{2,1,0:T(8,128)}, u32[]{:S(2)}) copy-start(f32[2,512,512]{2,1,0:T(8,128)} %param.15) | copy-start | bytes 6291460
  7.2 482.5 %all-reduce.2.cloned.1.call-start = ((), (), s32[]{:S(2)}) async-start(), calls=%async_computation | async-start | bytes 4194304 | tf_op jit(solution)/shard_map/psum | solution.py:147
  8.6 11.0 %collective-permute-start = (f32[2,128,512]{2,1,0:T(8,128)S(1)}, f32[2,128,512]{2,1,0:T(8,128)S(1)}, u32[]{:S(2)}, u32[]{:S(2)}) collective-permute-start(f32[2,128,512]{2,1,0:T(8,128)S(1)} %get-tuple-element.379), channel_id=1, source_target_pairs={{0,8},{8,16},{16,24},{24,32},{32,40},{40,48},{48,56},{56,64},{64,7... | collective-permute-start | bytes 1572872 | tf_op jit(solution)/shard_map/ppermute | solution.py:25
  13.6 10.5 %collective-permute-start.1 = (f32[2,128,512]{2,1,0:T(8,128)S(1)}, f32[2,128,512]{2,1,0:T(8,128)S(1)}, u32[]{:S(2)}, u32[]{:S(2)}) collective-permute-start(f32[2,128,512]{2,1,0:T(8,128)S(1)} %get-tuple-element.378), channel_id=1, source_target_pairs={{8,0},{16,8},{24,16},{32,24},{40,32},{48,40},{56,48},{64,56},{72,6... | collective-permute-start | bytes 1572872 | tf_op jit(solution)/shard_map/ppermute | solution.py:27
  24.1 1.7 copy-start.1
  25.8 7.7 %copy-start.5 = (s32[1,1,4,2]{2,3,1,0:T(2,128)S(1)}, s32[1,1,4,2]{2,3,1,0:T(2,128)}, u32[]{:S(2)}) copy-start(s32[1,1,4,2]{2,3,1,0:T(2,128)} %param.18) | copy-start | bytes 100
  27.0 14.6 %collective-permute-start.2 = (f32[2,768,128]{2,1,0:T(8,128)}, f32[2,768,128]{2,1,0:T(8,128)S(1)}, u32[]{:S(2)}, u32[]{:S(2)}) collective-permute-start(f32[2,768,128]{2,1,0:T(8,128)} %get-tuple-element.376), channel_id=1, source_target_pairs={{0,1},{1,2},{2,3},{3,4},{4,5},{5,6},{6,7},{8,9},{9,10},{10,11},{11... | collective-permute-start | bytes 2359304 | tf_op jit(solution)/shard_map/ppermute | solution.py:25
  30.3 15.5 %collective-permute-start.3 = (f32[2,768,128]{2,1,0:T(8,128)}, f32[2,768,128]{2,1,0:T(8,128)}, u32[]{:S(2)}, u32[]{:S(2)}) collective-permute-start(f32[2,768,128]{2,1,0:T(8,128)} %get-tuple-element.377), channel_id=1, source_target_pairs={{1,0},{2,1},{3,2},{4,3},{5,4},{6,5},{7,6},{9,8},{10,9},{11,10},{12... | collective-permute-start | bytes 2359304 | tf_op jit(solution)/shard_map/ppermute | solution.py:27
  31.6 14.2 %copy-start.2 = (f32[2,768,512]{2,1,0:T(8,128)S(1)}, f32[2,768,512]{2,1,0:T(8,128)}, u32[]{:S(2)}) copy-start(f32[2,768,512]{2,1,0:T(8,128)} %copy-done.1) | copy-start | bytes 9437188
  212.0 19.2 %collective-permute-start.4 = (f32[2,128,768]{2,1,0:T(8,128)}, f32[2,128,768]{2,1,0:T(8,128)S(1)}, u32[]{:S(2)}, u32[]{:S(2)}) collective-permute-start(f32[2,128,768]{2,1,0:T(8,128)} %get-tuple-element.373), channel_id=1, source_target_pairs={{8,0},{16,8},{24,16},{32,24},{40,32},{48,40},{56,48},{64,56},{72,6... | collective-permute-start | bytes 2359304 | tf_op jit(solution)/shard_map/ppermute | solution.py:14
  213.9 18.5 %collective-permute-start.5 = (f32[2,128,768]{2,1,0:T(8,128)S(1)}, f32[2,128,768]{2,1,0:T(8,128)S(1)}, u32[]{:S(2)}, u32[]{:S(2)}) collective-permute-start(f32[2,128,768]{2,1,0:T(8,128)S(1)} %get-tuple-element.372), channel_id=1, source_target_pairs={{0,8},{8,16},{16,24},{24,32},{32,40},{40,48},{48,56},{56,64},{64,7... | collective-permute-start | bytes 2359304 | tf_op jit(solution)/shard_map/ppermute | solution.py:14
  232.7 2.7 copy-start
  233.8 259.0 %collective-permute-start.6 = (f32[2,512,128]{2,1,0:T(8,128)}, f32[2,512,128]{2,1,0:T(8,128)S(1)}, u32[]{:S(2)}, u32[]{:S(2)}) collective-permute-start(f32[2,512,128]{2,1,0:T(8,128)} %get-tuple-element.375), channel_id=1, source_target_pairs={{1,0},{2,1},{3,2},{4,3},{5,4},{6,5},{7,6},{9,8},{10,9},{11,10},{12... | collective-permute-start | bytes 1572872 | tf_op jit(solution)/shard_map/ppermute | solution.py:14
  235.4 258.6 %collective-permute-start.7 = (f32[2,512,128]{2,1,0:T(8,128)}, f32[2,512,128]{2,1,0:T(8,128)S(1)}, u32[]{:S(2)}, u32[]{:S(2)}) collective-permute-start(f32[2,512,128]{2,1,0:T(8,128)} %get-tuple-element.374), channel_id=1, source_target_pairs={{0,1},{1,2},{2,3},{3,4},{4,5},{5,6},{6,7},{8,9},{9,10},{10,11},{11... | collective-permute-start | bytes 1572872 | tf_op jit(solution)/shard_map/ppermute | solution.py:14
  494.1 1.3 copy-start.4
Sparse Core Ops, SparseCore 0:
  226.2 263.4 all-reduce.1
where the time goes:
time: 505 us; the launch traced here: 502 us
  waiting for transfers between devices  274 us (54%)
  matrix products  83.6 us (17%)
  local copies, waits for them, and re-layouts  52.9 us (10%)
  other arithmetic  31.6 us (6%)
  starting transfers between devices  27.7 us (5%)
  loops' own time  18.2 us (4%)
  between operations  14.3 us (3%)
    psum x1, waiting for transfers between devices, on_device(): probe_total = lax.psum(probe_acc, ('rows', 'cols'))  250 us
    dot_general x32, matrix products, batch_right(): jnp.einsum('mab,bc->mac', values, table, preferred_element_type=jnp.float32)  43.1 us
    dot_general x32, matrix products, batch_left(): jnp.einsum('ab,mbc->mac', table, values, preferred_element_type=jnp.float32)  40.4 us
    dynamic_update_slice x4, local copies, waits for them, and re-layouts, visit(): lax.dynamic_update_slice(gradient, before + object_term, (anchor, top_row...  25.8 us
    another operation x1, loops' own time, on_device(): lax.fori_loop(0, slot_total, lambda slot_id, state: visit(slot_id, state)...  18.2 us
    ppermute x4, starting transfers between devices, shifted(): lax.ppermute(value, axis, [(source, source + steps) for source in range(l...  16.3 us
    ppermute x2, waiting for transfers between devices, extended(): lax.ppermute(tail, axis, [(i, (i + 1) % count) for i in range(ends)])  12.3 us
    add x4, other arithmetic, visit(): return (gradient, probe_acc + probe_term)  11.4 us
  transfers between devices with their start and end apart: 9, of which 6 were waited for; matrix products, arithmetic and copies ran while one was open for 3% of the time, Pallas kernels for 0%

commit v1 on v0

v1 whole, which is shorter than its diff:
```python
import functools
import math

import jax
import jax.numpy as jnp
from jax import lax
from jax.experimental import pallas as pl
from jax.experimental.pallas import tpu as pltpu
from jax.sharding import PartitionSpec as P

MESH = pl.DeviceIdType.MESH
background = 1.0
S = 256
RIM = 128
T = 512
E = T + 2 * RIM
M = 4
SLOTS = 4
WROWS, WCOLS = S + 8, S + 128


def dft_table(wave_size):
    ramp = jnp.arange(wave_size, dtype=jnp.int32)
    phases = ramp[:, None] * ramp[None, :] % wave_size
    angles = phases.astype(jnp.float32) * (2.0 * math.pi / wave_size)
    scaling = 1.0 / math.sqrt(wave_size)
    cos_t = (jnp.cos(angles) * scaling).astype(jnp.bfloat16)
    sin_t = (jnp.sin(angles) * scaling).astype(jnp.bfloat16)
    return jnp.concatenate(
        [jnp.concatenate([cos_t, sin_t], axis=1), jnp.concatenate([-sin_t, cos_t], axis=1)], axis=0
    )


def halo_kernel(tile, out, padded, send_sem, recv_sem, own_sem, out_sem):
    r, c = lax.axis_index("rows"), lax.axis_index("cols")
    n_r, n_c = lax.axis_size("rows"), lax.axis_size("cols")
    up, down, left, right = r > 0, r < n_r - 1, c > 0, c < n_c - 1
    to_up, to_down, to_left, to_right = (r - 1, c), (r + 1, c), (r, c - 1), (r, c + 1)
    sides = ((up, to_up), (down, to_down), (left, to_left), (right, to_right))
    lo, mid, hi = pl.ds(0, RIM), pl.ds(RIM, T), pl.ds(RIM + T, RIM)

    center = padded.at[:, mid, mid]
    own = pltpu.make_async_copy(tile, center, own_sem)
    own.start()
    barrier = pltpu.get_barrier_semaphore()
    for there, device in sides:

        @pl.when(there)
        def _(device=device):
            pl.semaphore_signal(barrier, inc=1, device_id=device, device_id_type=MESH)

    own.wait()
    pl.semaphore_wait(barrier, sum(jnp.where(there, 1, 0) for there, _ in sides))

    def copy(index, src, dst, device):
        return pltpu.make_async_remote_copy(
            src_ref=src,
            dst_ref=dst,
            send_sem=send_sem.at[index],
            recv_sem=recv_sem.at[index],
            device_id=device,
            device_id_type=MESH,
        )

    near, far = pl.ds(RIM, RIM), pl.ds(T, RIM)
    spans = (pl.ds(RIM, RIM), pl.ds(T, RIM), pl.ds(2 * RIM, T - 2 * RIM))
    to_l = [copy(i, padded.at[:, spans[i], near], padded.at[:, spans[i], hi], to_left) for i in range(3)]
    to_r = [copy(3 + i, padded.at[:, spans[i], far], padded.at[:, spans[i], lo], to_right) for i in range(3)]
    to_u = copy(6, padded.at[:, near, mid], padded.at[:, hi, mid], to_up)
    to_d = copy(7, padded.at[:, far, mid], padded.at[:, lo, mid], to_down)
    c_ul = copy(8, padded.at[:, near, lo], padded.at[:, hi, lo], to_up)
    c_ur = copy(9, padded.at[:, near, hi], padded.at[:, hi, hi], to_up)
    c_dl = copy(10, padded.at[:, far, lo], padded.at[:, lo, lo], to_down)
    c_dr = copy(11, padded.at[:, far, hi], padded.at[:, lo, hi], to_down)

    def starts(there, *some):
        @pl.when(there)
        def _():
            for one in some:
                one.start()

    for i in range(3):
        starts(left, to_l[i])
        starts(right, to_r[i])
        if i == 0:
            starts(up, to_u)
            starts(down, to_d)

    stored = []

    def store(rows, cols):
        one = pltpu.make_async_copy(padded.at[:, rows, cols], out.at[:, rows, cols], out_sem.at[len(stored)])
        one.start()
        stored.append(one)

    def arrived(there, rows, cols, *some):
        @pl.when(there)
        def _():
            for one in some:
                one.wait_recv()

        @pl.when(jnp.logical_not(there))
        def _():
            padded[:, rows, cols] = jnp.zeros((2, rows.size, cols.size), jnp.float32)

    store(mid, mid)
    arrived(left, near, lo, to_r[0])
    starts(left & up, c_ul)
    arrived(right, near, hi, to_l[0])
    starts(right & up, c_ur)
    arrived(left, far, lo, to_r[1])
    starts(left & down, c_dl)
    arrived(right, far, hi, to_l[1])
    starts(right & down, c_dr)
    arrived(up, lo, mid, to_d)
    store(lo, mid)
    arrived(down, hi, mid, to_u)
    store(hi, mid)
    arrived(up & left, lo, lo, c_dl)
    store(lo, lo)
    arrived(up & right, lo, hi, c_dr)
    store(lo, hi)
    arrived(down & left, hi, lo, c_ul)
    store(hi, lo)
    arrived(down & right, hi, hi, c_ur)
    store(hi, hi)
    arrived(left, spans[2], lo, to_r[2])
    store(mid, lo)
    arrived(right, spans[2], hi, to_l[2])
    store(mid, hi)
    for one in stored:
        one.wait()

    for there, some in (
        (left, to_l),
        (right, to_r),
        (up, [to_u]),
        (down, [to_d]),
        (up & left, [c_ul]),
        (up & right, [c_ur]),
        (down & left, [c_dl]),
        (down & right, [c_dr]),
    ):

        @pl.when(there)
        def _(some=some):
            for one in some:
                one.wait_send()


def halo(tile):
    return pl.pallas_call(
        halo_kernel,
        out_shape=jax.ShapeDtypeStruct((2, E, E), jnp.float32),
        in_specs=[pl.BlockSpec(memory_space=pl.ANY)],
        out_specs=pl.BlockSpec(memory_space=pl.ANY),
        scratch_shapes=[
            pltpu.VMEM((2, E, E), jnp.float32),
            pltpu.SemaphoreType.DMA((12,)),
            pltpu.SemaphoreType.DMA((12,)),
            pltpu.SemaphoreType.DMA,
            pltpu.SemaphoreType.DMA((9,)),
        ],
        compiler_params=pltpu.CompilerParams(collective_id=0, has_side_effects=True, vmem_limit_bytes=32 << 20),
    )(tile)


STEP = 32


def dot(a, b):
    return jnp.dot(a, b, preferred_element_type=jnp.float32)


def slots_kernel(
    corners, live, padded, probe, photons, fwd, bwd, grad, pacc, window, counts, patch, terms, rows_in, cols_in, wave, win_sem, cnt_sem
):
    def box(slot):
        top, left = corners[slot, 0] + RIM, corners[slot, 1] + RIM
        top0 = pl.multiple_of(jnp.minimum(top // 8 * 8, E - WROWS), 8)
        left0 = pl.multiple_of(jnp.minimum(left // 128 * 128, E - WCOLS), 128)
        return top0, left0, top - top0, left - left0

    def fetches(slot):
        top0, left0, _, _ = box(slot)
        return (
            pltpu.make_async_copy(
                padded.at[:, pl.ds(top0, WROWS), pl.ds(left0, WCOLS)], window.at[slot], win_sem.at[slot]
            ),
            pltpu.make_async_copy(photons.at[slot], counts.at[slot], cnt_sem.at[slot]),
        )

    for slot in range(SLOTS):
        for one in fetches(slot):
            one.start()
    grad[...] = jnp.zeros_like(grad)
    pacc[...] = jnp.zeros_like(pacc)
    lane = lax.broadcasted_iota(jnp.int32, (8, 128), 1)
    sublane = lax.broadcasted_iota(jnp.int32, (8, 128), 0)
    nothing = jnp.zeros((8, 128), jnp.float32)

    def visit(slot, carry):
        top0, left0, down, over = box(slot)
        for one in fetches(slot):
            one.wait()
        back_by, ahead_by = lax.rem(128 - over, 128), lax.rem(over, 128)
        up_by, down_by = lax.rem(8 - down, 8), lax.rem(down, 8)
        for k in range(2):
            before = None
            for i in range(WROWS // 8):
                a, b, d = (
                    pltpu.roll(window[slot, k, 8 * i : 8 * i + 8, 128 * j : 128 * j + 128], back_by, 1) for j in range(3)
                )
                keep = lane < 128 - over
                now = tuple(pltpu.roll(v, up_by, 0) for v in (jnp.where(keep, a, b), jnp.where(keep, b, d)))
                if i:
                    for j in range(2):
                        patch[k, 8 * i - 8 : 8 * i, 128 * j : 128 * j + 128] = jnp.where(
                            sublane < 8 - down, before[j], now[j]
                        )
                before = now
        for m in range(M):
            for r in range(0, S, STEP):
                here = pl.ds(r, STEP)
                o_re, o_im = patch[0, here, :], patch[1, here, :]
                p_re, p_im = probe[m, 0, here, :], probe[m, 1, here, :]
                rows_in[m, r : r + STEP, :] = (p_re * o_re - p_im * o_im).astype(jnp.bfloat16)
                rows_in[m, S + r : S + r + STEP, :] = (p_re * o_im + p_im * o_re).astype(jnp.bfloat16)
            half = dot(fwd[...], rows_in[m])
            cols_in[m, :, 0:S] = half[0:S].astype(jnp.bfloat16)
            cols_in[m, :, S:] = half[S:].astype(jnp.bfloat16)
            wave[m] = dot(cols_in[m], bwd[...])
        for r in range(0, S, STEP):
            here = pl.ds(r, STEP)
            total = None
            for m in range(M):
                w_re, w_im = wave[m, here, 0:S], wave[m, here, S:]
                term = w_re * w_re + w_im * w_im
                total = term if m == 0 else total + term
            factor = 1.0 - counts[slot, here, :].astype(jnp.float32) / (total + background)
            for m in range(M):
                rows_in[m, r : r + STEP, :] = (factor * wave[m, here, 0:S]).astype(jnp.bfloat16)
                rows_in[m, S + r : S + r + STEP, :] = (factor * wave[m, here, S:]).astype(jnp.bfloat16)
        for m in range(M):
            back = dot(bwd[...], rows_in[m])
            cols_in[m, :, 0:S] = back[0:S].astype(jnp.bfloat16)
            cols_in[m, :, S:] = back[S:].astype(jnp.bfloat16)
            wave[m] = dot(cols_in[m], fwd[...])
        for r in range(0, S, STEP):
            here = pl.ds(r, STEP)
            o_re, o_im = patch[0, here, :], patch[1, here, :]
            t_re = t_im = None
            for m in range(M):
                c_re, c_im = wave[m, here, 0:S], wave[m, here, S:]
                p_re, p_im = probe[m, 0, here, :], probe[m, 1, here, :]
                a_re, a_im = p_re * c_re + p_im * c_im, p_re * c_im - p_im * c_re
                t_re, t_im = (a_re, a_im) if m == 0 else (t_re + a_re, t_im + a_im)
                pacc[m, 0, here, :] += o_re * c_re + o_im * c_im
                pacc[m, 1, here, :] += o_re * c_im - o_im * c_re
            terms[0, here, :], terms[1, here, :] = t_re, t_im
        inside = lane >= over
        for k in range(2):
            before = (nothing, nothing)
            for i in range(WROWS // 8):
                now = (nothing, nothing)
                if i < S // 8:
                    now = tuple(
                        pltpu.roll(terms[k, 8 * i : 8 * i + 8, 128 * j : 128 * j + 128], down_by, 0) for j in range(2)
                    )
                a, b = (pltpu.roll(jnp.where(sublane >= down, now[j], before[j]), ahead_by, 1) for j in range(2))
                before = now
                spread = (jnp.where(inside, a, 0.0), jnp.where(inside, b, a), jnp.where(inside, 0.0, b))
                rows = pl.ds(pl.multiple_of(top0 + 8 * i, 8), 8)
                for j in range(3):
                    grad[k, rows, pl.ds(pl.multiple_of(left0 + j * 128, 128), 128)] += spread[j]
        return carry

    lax.fori_loop(0, live[0, 0], visit, 0)

    def drain(slot, carry):
        for one in fetches(slot):
            one.wait()
        return carry

    lax.fori_loop(live[0, 0], SLOTS, drain, 0)


def slots(padded, probe, photons, corners, live):
    fwd = dft_table(S)
    vmem, smem, anywhere = (pl.BlockSpec(memory_space=m) for m in (pltpu.VMEM, pltpu.SMEM, pl.ANY))
    return pl.pallas_call(
        slots_kernel,
        out_shape=(
            jax.ShapeDtypeStruct((2, E, E), jnp.float32),
            jax.ShapeDtypeStruct((M, 2, S, S), jnp.float32),
        ),
        in_specs=[smem, smem, anywhere, vmem, anywhere, vmem, vmem],
        out_specs=(vmem, vmem),
        scratch_shapes=[
            pltpu.VMEM((SLOTS, 2, WROWS, WCOLS), jnp.float32),
            pltpu.VMEM((SLOTS, S, S), jnp.int32),
            pltpu.VMEM((2, S, S), jnp.float32),
            pltpu.VMEM((2, S, S), jnp.float32),
            pltpu.VMEM((M, 2 * S, S), jnp.bfloat16),
            pltpu.VMEM((M, S, 2 * S), jnp.bfloat16),
            pltpu.VMEM((M, S, 2 * S), jnp.float32),
            pltpu.SemaphoreType.DMA((SLOTS,)),
            pltpu.SemaphoreType.DMA((SLOTS,)),
        ],
        compiler_params=pltpu.CompilerParams(vmem_limit_bytes=48 << 20),
    )(corners, live, padded, probe, photons, fwd, fwd.T)


GROUPS = M * 2 * S // 8
HALF = GROUPS // 2
PARTS = ((0, 64, ("x", "z", "y")), (64, 32, ("y", "z", "x")), (96, 32, ("z", "x", "y")))
AXES = {"x": 4, "y": 4, "z": 8}


def sums_kernel(grad, pacc, core_out, probe_out, above, below, left_in, right_in, acc, from_twin, *rest):
    n_parts = len(PARTS)
    ins = [rest[3 * i : 3 * i + 3] for i in range(n_parts)]
    sums = [rest[3 * n_parts + 2 * i : 3 * n_parts + 2 * i + 2] for i in range(n_parts)]
    send_sem, recv_sem = rest[5 * n_parts :]
    r, c = lax.axis_index("rows"), lax.axis_index("cols")
    n_r, n_c = lax.axis_size("rows"), lax.axis_size("cols")
    up, down, left, right = r > 0, r < n_r - 1, c > 0, c < n_c - 1
    to_up, to_down, to_left, to_right = (r - 1, c), (r + 1, c), (r, c - 1), (r, c + 1)
    core = r % 2
    at = {"x": r // 16 * 2 + c // 4, "y": c % 4, "z": r // 2 % 8}
    twin = (r + 1 - 2 * core, c)

    def peer(axis, k):
        place = dict(at)
        place[axis] = (at[axis] + k) % AXES[axis]
        return (place["x"] // 2 * 16 + place["z"] * 2 + core, place["x"] % 2 * 4 + place["y"])

    sides = ((up, to_up), (down, to_down), (left, to_left), (right, to_right))
    peers = [twin] + [peer(axis, k) for axis in AXES for k in range(1, AXES[axis])]
    barrier = pltpu.get_barrier_semaphore()
    for device in peers:
        pl.semaphore_signal(barrier, inc=1, device_id=device, device_id_type=MESH)
    for there, device in sides:

        @pl.when(there)
        def _(device=device):
            pl.semaphore_signal(barrier, inc=1, device_id=device, device_id_type=MESH)

    pl.semaphore_wait(barrier, len(peers) + sum(jnp.where(there, 1, 0) for there, _ in sides))

    count = [0]

    def copy(src, dst, device):
        index = count[0]
        count[0] += 1
        return pltpu.make_async_remote_copy(
            src_ref=src,
            dst_ref=dst,
            send_sem=send_sem.at[index],
            recv_sem=recv_sem.at[index],
            device_id=device,
            device_id_type=MESH,
        )

    sent = []

    def go(some):
        for one in some:
            one.start()
        sent.extend(some)
        return some

    first = HALF * core
    other = HALF * (1 - core)
    stage0 = [
        go([copy(pacc.at[pl.ds(other + p0, size)], from_twin.at[pl.ds(p0, size)], twin)])[0] for p0, size, _ in PARTS
    ]
    lo, hi = pl.ds(0, RIM), pl.ds(RIM + T, RIM)
    bands = (pl.ds(0, RIM), pl.ds(RIM + T, RIM), pl.ds(RIM, T))
    to_u = [copy(grad.at[:, lo, b], below.at[:, :, b], to_up) for b in bands]
    to_d = [copy(grad.at[:, hi, b], above.at[:, :, b], to_down) for b in bands]
    spans = ((2 * RIM, T - 2 * RIM), (RIM, RIM), (T, RIM))
    to_l = [copy(grad.at[:, pl.ds(s, n), lo], right_in.at[:, pl.ds(s - RIM, n), :], to_left) for s, n in spans]
    to_r = [copy(grad.at[:, pl.ds(s, n), hi], left_in.at[:, pl.ds(s - RIM, n), :], to_right) for s, n in spans]

    def when_start(there, some):
        @pl.when(there)
        def _():
            for one in some:
                one.start()

    when_start(up, to_u)
    when_start(down, to_d)
    when_start(left, to_l[:1])
    when_start(right, to_r[:1])

    stage1 = []
    for i, (p0, size, axes) in enumerate(PARTS):
        stage0[i].wait_recv()
        acc[pl.ds(p0, size)] = pacc[pl.ds(first + p0, size)] + from_twin[pl.ds(p0, size)]
        n = AXES[axes[0]]
        s = size // n
        some = []
        for k in range(1, n):
            to = (at[axes[0]] + k) % n
            some.append(copy(acc.at[pl.ds(p0 + s * to, s)], ins[i][0].at[k - 1], peer(axes[0], k)))
        stage1.append(go(some))

    @pl.when(up)
    def _():
        for one in to_d[:2]:
            one.wait_recv()
        grad[:, RIM : 2 * RIM, 0:RIM] += above[:, :, 0:RIM]
        grad[:, RIM : 2 * RIM, RIM + T :] += above[:, :, RIM + T :]

    when_start(left, to_l[1:2])
    when_start(right, to_r[1:2])

    @pl.when(down)
    def _():
        for one in to_u[:2]:
            one.wait_recv()
        grad[:, T : T + RIM, 0:RIM] += below[:, :, 0:RIM]
        grad[:, T : T + RIM, RIM + T :] += below[:, :, RIM + T :]

    when_start(left, to_l[2:])
    when_start(right, to_r[2:])

    stage2 = []
    for i, (p0, size, axes) in enumerate(PARTS):
        n = AXES[axes[0]]
        s = size // n
        for one in stage1[i]:
            one.wait_recv()
        total = acc[pl.ds(p0 + s * at[axes[0]], s)]
        for k in range(n - 1):
            total = total + ins[i][0][k]
        sums[i][0][...] = total
        n2 = AXES[axes[1]]
        s2 = s // n2
        some = []
        for k in range(1, n2):
            to = (at[axes[1]] + k) % n2
            some.append(copy(sums[i][0].at[pl.ds(s2 * to, s2)], ins[i][1].at[k - 1], peer(axes[1], k)))
        stage2.append(go(some))

    stage3 = []
    for i, (p0, size, axes) in enumerate(PARTS):
        n2 = AXES[axes[1]]
        s2 = size // AXES[axes[0]] // n2
        for one in stage2[i]:
            one.wait_recv()
        total = sums[i][0][pl.ds(s2 * at[axes[1]], s2)]
        for k in range(n2 - 1):
            total = total + ins[i][1][k]
        mine = ins[i][2].at[at[axes[2]]]
        sums[i][1][...] = total
        ins[i][2][at[axes[2]]] = total
        stage3.append(go([copy(sums[i][1], mine, peer(axes[2], k)) for k in range(1, AXES[axes[2]])]))

    scale = 1.0 / math.sqrt(n_r * n_c)
    gather2 = []
    for i, (p0, size, axes) in enumerate(PARTS):
        s = size // AXES[axes[0]]
        s2 = s // AXES[axes[1]]
        for one in stage3[i]:
            one.wait_recv()
        total = ins[i][2][0]
        for j in range(1, AXES[axes[2]]):
            total = total + ins[i][2][j]
        place = pl.ds(first + p0 + s * at[axes[0]] + s2 * at[axes[1]], s2)
        probe_out[place] = total * scale
        block = probe_out.at[place]
        gather2.append(go([copy(block, block, peer(axes[1], k)) for k in range(1, AXES[axes[1]])]))
    gather1 = []
    for i, (p0, size, axes) in enumerate(PARTS):
        s = size // AXES[axes[0]]
        for one in gather2[i]:
            one.wait_recv()
        block = probe_out.at[pl.ds(first + p0 + s * at[axes[0]], s)]
        gather1.append(go([copy(block, block, peer(axes[0], k)) for k in range(1, AXES[axes[0]])]))
    gather0 = []
    for i, (p0, size, axes) in enumerate(PARTS):
        for one in gather1[i]:
            one.wait_recv()
        block = probe_out.at[pl.ds(first + p0, size)]
        gather0.append(go([copy(block, block, twin)])[0])

    core_out[...] = grad[:, RIM : RIM + T, RIM : RIM + T]

    @pl.when(up)
    def _():
        to_d[2].wait_recv()
        core_out[:, 0:RIM, :] += above[:, :, RIM : RIM + T]

    @pl.when(down)
    def _():
        to_u[2].wait_recv()
        core_out[:, T - RIM :, :] += below[:, :, RIM : RIM + T]

    @pl.when(left)
    def _():
        for one in to_r:
            one.wait_recv()
        core_out[:, :, 0:RIM] += left_in[...]

    @pl.when(right)
    def _():
        for one in to_l:
            one.wait_recv()
        core_out[:, :, T - RIM :] += right_in[...]

    for there, some in ((up, to_u), (down, to_d), (left, to_l), (right, to_r)):

        @pl.when(there)
        def _(some=some):
            for one in some:
                one.wait_send()

    for one in gather0:
        one.wait_recv()
    for one in sent:
        one.wait_send()


def sums(grad, pacc):
    ins, parts = [], []
    copies = 2 * len(PARTS) + 12
    for _p0, size, axes in PARTS:
        n = [AXES[a] for a in axes]
        s = size // n[0]
        s2 = s // n[1]
        ins += [
            pltpu.VMEM((n[0] - 1, s, 8, S), jnp.float32),
            pltpu.VMEM((n[1] - 1, s2, 8, S), jnp.float32),
            pltpu.VMEM((n[2], s2, 8, S), jnp.float32),
        ]
        parts += [pltpu.VMEM((s, 8, S), jnp.float32), pltpu.VMEM((s2, 8, S), jnp.float32)]
        copies += 2 * (n[0] + n[1] - 2) + n[2] - 1
    vmem = pl.BlockSpec(memory_space=pltpu.VMEM)
    core, probe_grad = pl.pallas_call(
        sums_kernel,
        out_shape=(
            jax.ShapeDtypeStruct((2, T, T), jnp.float32),
            jax.ShapeDtypeStruct((GROUPS, 8, S), jnp.float32),
        ),
        in_specs=[vmem, vmem],
        out_specs=(vmem, vmem),
        scratch_shapes=[
            pltpu.VMEM((2, RIM, E), jnp.float32),
            pltpu.VMEM((2, RIM, E), jnp.float32),
            pltpu.VMEM((2, T, RIM), jnp.float32),
            pltpu.VMEM((2, T, RIM), jnp.float32),
            pltpu.VMEM((HALF, 8, S), jnp.float32),
            pltpu.VMEM((HALF, 8, S), jnp.float32),
            *ins,
            *parts,
            pltpu.SemaphoreType.DMA((copies,)),
            pltpu.SemaphoreType.DMA((copies,)),
        ],
        compiler_params=pltpu.CompilerParams(collective_id=1, has_side_effects=True, vmem_limit_bytes=48 << 20),
    )(grad, pacc.reshape(GROUPS, 8, S))
    return core, probe_grad.reshape(M, 2, S, S)


def on_device(object_field, probe, photons, positions, live_counts):
    padded = halo(object_field)
    grad, pacc = slots(padded, probe, photons[0, 0], positions[0, 0], live_counts)
    return sums(grad, pacc)


def solution(mesh):
    in_specs = (
        P(None, "rows", "cols"),
        P(),
        P("rows", "cols", None, None, None),
        P("rows", "cols", None, None),
        P("rows", "cols"),
    )
    out_specs = (P(None, "rows", "cols"), P())
    return jax.shard_map(on_device, mesh=mesh, in_specs=in_specs, out_specs=out_specs, check_vma=False)
```

time: 505 us -> 120 us (0.24)
  waiting for transfers between devices: 274 us -> 0 us
  Pallas kernels: 0 us -> 107 us
  matrix products: 83.6 us -> 0 us
  local copies, waits for them, and re-layouts: 52.9 us -> 8.11 us
  other arithmetic: 31.6 us -> 2.96 us
  starting transfers between devices: 27.7 us -> 0 us
  loops' own time: 18.2 us -> 0 us
  between operations: 14.3 us -> 1.5 us
    psum x1 -> x0, waiting for transfers between devices: 250 us -> none  [on_device(): probe_total = lax.psum(probe_acc, ('rows', 'cols'))]
    pallas_call x0 -> x3, Pallas kernels: none -> 107 us  [the longest x1 67.6 us: sums(): pl.pallas_call(sums_kernel, out_shape=(jax.ShapeDtypeStruct((2, T, T), jn...]
    dot_general x64 -> x0, matrix products: 83.6 us -> none  [the longest x32 43.1 us: batch_right(): jnp.einsum('mab,bc->mac', values, table, preferred_element_type=jnp.float32)]
    ppermute x8 -> x0, starting transfers between devices: 27.6 us -> none  [the longest x4 16.3 us: shifted(): lax.ppermute(value, axis, [(source, source + steps) for source in range(l...]
    dynamic_update_slice x4 -> x0, local copies, waits for them, and re-layouts: 25.8 us -> none  [visit(): lax.dynamic_update_slice(gradient, before + object_term, (anchor, top_row...]
    ppermute x8 -> x0, waiting for transfers between devices: 23.7 us -> none  [the longest x2 12.3 us: extended(): lax.ppermute(tail, axis, [(i, (i + 1) % count) for i in range(ends)])]
    another operation x1 -> x0, loops' own time: 18.2 us -> none  [on_device(): lax.fori_loop(0, slot_total, lambda slot_id, state: visit(slot_id, state)...]
    add x9 -> x0, other arithmetic: 17 us -> none  [the longest x4 11.4 us: visit(): return (gradient, probe_acc + probe_term)]
  transfers between devices with their start and end apart: 9 -> 0, of which waited for: 6 -> 0; matrix products, arithmetic and copies ran while one was open for 3% -> 0% of each run, Pallas kernels for 0% -> 0%
where the time goes in v1:
time: 120 us
  Pallas kernels  107 us (89%)
  local copies, waits for them, and re-layouts  8.11 us (7%)
  other arithmetic  2.96 us (2%)
  between operations  1.5 us (1%)
    pallas_call x1, Pallas kernels, sums(): pl.pallas_call(sums_kernel, out_shape=(jax.ShapeDtypeStruct((2, T, T), jn...  67.6 us
    pallas_call x1, Pallas kernels, slots(): pl.pallas_call(slots_kernel, out_shape=(jax.ShapeDtypeStruct((2, E, E), j...  22.7 us
    pallas_call x1, Pallas kernels, halo(): pl.pallas_call(halo_kernel, out_shape=jax.ShapeDtypeStruct((2, E, E), jnp...  16.7 us
    unnamed x10, local copies, waits for them, and re-layouts  6.1 us

profile of v1, /device:TPU:1, one launch (start us, length us, event | category | flops | bytes accessed | tf_op | source)
XLA Modules:
  0.0 119.6 jit_solution(10128989245164768227)
XLA Ops:
  0.6 0.0 copy-start.1
  1.4 0.8 copy.7.corners
  2.2 1.0 fusion.6
  3.2 1.1 multiply_convert_fusion
  4.3 0.9 fusion.7
  5.2 1.3 %copy.8.fwd = bf16[512,512]{1,0:T(8,128)(2,1)S(1)} copy(bf16[512,512]{0,1:T(8,128)(2,1)} %get-tuple-element.11) | data formatting | bytes 1048576 | tf_op jit(solution)/shard_map/concatenate | solution.py:29
  6.4 0.0 copy-done.1
  6.4 0.0 copy-start.3
  6.4 16.7 %shard_map.68.padded = f32[2,768,768]{2,1,0:T(8,128)S(1)} custom-call(f32[2,512,512]{2,1,0:T(8,128)S(1)} %copy-done.1), custom_call_target="tpu_custom_call" | custom-call | tf_op jit(solution)/shard_map/pallas_call | solution.py:152
  23.2 0.0 copy-start
  23.2 2.1 %copy-done = f32[2,768,768]{2,1,0:T(8,128)} copy-done((f32[2,768,768]{2,1,0:T(8,128)}, f32[2,768,768]{2,1,0:T(8,128)S(1)}, u32[]{:S(2)}) %copy-start) | copy-done | bytes 4718616
  25.3 0.0 copy-done.3
  25.3 22.7 %shard_map.69 = (f32[2,768,768]{2,1,0:T(8,128)}, f32[4,2,256,256]{3,2,1,0:T(8,128)S(1)}) custom-call(s32[4,2]{1,0:T(4,128)S(1)} %copy.7.corners, s32[1,1]{1,0:T(1,128)S(6)} %copy.11.live, f32[2,768,768]{2,1,0:T(8,128)} %copy-done, f32[4,2,256,256]{3,2,1,0:T(8,128)} %probe.1, s32[4,256,256]{2,1,0:T(8,128)S(1)} %bitcast.8, bf16[512,512]{1,0:T(8,128)(2,1)S(1)} %copy.8.fwd, ...), custom_call_target="tpu_custom_call" | custom-call | tf_op jit(solution)/shard_map/pallas_call | solution.py:291
  48.1 0.0 copy-start.2
  48.1 1.3 %copy-done.2 = f32[4,2,256,256]{3,2,1,0:T(8,128)} copy-done((f32[4,2,256,256]{3,2,1,0:T(8,128)}, f32[4,2,256,256]{3,2,1,0:T(8,128)S(1)}, u32[]{:S(2)}) %copy-start.2) | copy-done | bytes 2097176
  49.4 67.6 %shard_map.70 = (f32[2,512,512]{2,1,0:T(8,128)S(1)}, f32[256,8,256]{2,1,0:T(8,128)S(1)}) custom-call(f32[2,768,768]{2,1,0:T(8,128)} %get-tuple-element.6.grad, f32[256,8,256]{2,1,0:T(8,128)} %bitcast.6), custom_call_target="tpu_custom_call" | custom-call | tf_op jit(solution)/shard_map/pallas_call | solution.py:541
  117.0 1.3 %copy.12 = f32[2,512,512]{2,1,0:T(8,128)} copy(f32[2,512,512]{2,1,0:T(8,128)S(1)} %get-tuple-element.16) | data formatting | bytes 4194304
  118.3 1.3 %copy.13 = f32[4,2,256,256]{3,2,1,0:T(8,128)} copy(f32[4,2,256,256]{3,2,1,0:T(8,128)S(1)} %bitcast.7) | data formatting | bytes 4194304
Async XLA Ops:
  0.6 5.8 %copy-start.1 = (f32[2,512,512]{2,1,0:T(8,128)S(1)}, f32[2,512,512]{2,1,0:T(8,128)}, u32[]{:S(2)}) copy-start(f32[2,512,512]{2,1,0:T(8,128)} %tile.1) | copy-start | bytes 6291460
  6.4 18.9 %copy-start.3 = (s32[1,1,4,256,256]{4,3,2,1,0:T(8,128)S(1)}, s32[1,1,4,256,256]{4,3,2,1,0:T(8,128)}, u32[]{:S(2)}) copy-start(s32[1,1,4,256,256]{4,3,2,1,0:T(8,128)} %param.7) | copy-start | bytes 3145732
  23.2 2.1 %copy-start = (f32[2,768,768]{2,1,0:T(8,128)}, f32[2,768,768]{2,1,0:T(8,128)S(1)}, u32[]{:S(2)}) copy-start(f32[2,768,768]{2,1,0:T(8,128)S(1)} %shard_map.68.padded) | copy-start | bytes 14155780
  48.1 1.3 %copy-start.2 = (f32[4,2,256,256]{3,2,1,0:T(8,128)}, f32[4,2,256,256]{3,2,1,0:T(8,128)S(1)}, u32[]{:S(2)}) copy-start(f32[4,2,256,256]{3,2,1,0:T(8,128)S(1)} %get-tuple-element.7) | copy-start | bytes 6291460

commit v2 on v0

v2 whole, which is shorter than its diff:
```python
import math

import jax
import jax.numpy as jnp
import numpy as np
from jax import lax
from jax.experimental import pallas as pl
from jax.experimental.pallas import tpu as pltpu
from jax.sharding import PartitionSpec as P

MESH = pl.DeviceIdType.MESH
background = 1.0
S = 256
RIM = 128
T = 512
E = T + 2 * RIM
M = 4
SLOTS = 4
WROWS, WCOLS = S // 8 + 1, S // 128 + 1
ROWS, COLS = E // 8 + 1, E // 128 + 1
STEP = 32
GROUPS = M * 2 * S // 8
PER_MODE = GROUPS // M
PART = PER_MODE // 2
AXES = {"x": 4, "y": 4, "z": 8}
ORDERS = (("y", "x", "z"), ("x", "y", "z"), ("y", "x", "z"), ("x", "y", "z"))
N_SUM = sum(2 + 2 * (AXES[a] - 1) + 2 * (AXES[b] - 1) + AXES[d] - 1 for a, b, d in ORDERS)
N_COPIES = 24 + 48 + N_SUM


def dft_table(wave_size):
    ramp = np.arange(wave_size, dtype=np.int32)
    phases = ramp[:, None] * ramp[None, :] % wave_size
    angles = phases.astype(np.float32) * np.float32(2.0 * math.pi / wave_size)
    scaling = np.float32(1.0 / math.sqrt(wave_size))
    cos_t = (np.cos(angles) * scaling).astype(jnp.bfloat16)
    sin_t = (np.sin(angles) * scaling).astype(jnp.bfloat16)
    return np.block([[cos_t, sin_t], [-sin_t, cos_t]])


def dot(a, b):
    return jnp.dot(a, b, preferred_element_type=jnp.float32)


def box(corners, slot):
    top, left = corners[0, slot] + RIM, corners[1, slot] + RIM
    shift = lax.shift_right_logical
    return shift(top, 3), shift(left, 7), lax.bitwise_and(top, 7), lax.bitwise_and(left, 127)


def forward(slot, corners, live, padded, probe, counts, fwd, bwd, patch, rows_in, cols_in, wave):
    lane = lax.broadcasted_iota(jnp.int32, (8, 128), 1)
    sublane = lax.broadcasted_iota(jnp.int32, (8, 128), 0)
    top0, left0, down, over = box(corners, slot)
    back_by, up_by = lax.bitwise_and(128 - over, 127), lax.bitwise_and(8 - down, 7)
    keep = lane < 128 - over
    for k in range(2):
        before = None
        for i in range(WROWS):
            a, b, d = (pltpu.roll(padded[k, top0 + i, left0 + j], back_by, 1) for j in range(3))
            now = tuple(pltpu.roll(v, up_by, 0) for v in (jnp.where(keep, a, b), jnp.where(keep, b, d)))
            if i:
                for j in range(2):
                    patch[slot, k, 8 * i - 8 : 8 * i, 128 * j : 128 * j + 128] = jnp.where(
                        sublane < 8 - down, before[j], now[j]
                    )
            before = now
    for m in range(M):
        for r in range(0, S, STEP):
            here = pl.ds(r, STEP)
            o_re, o_im = patch[slot, 0, here, :], patch[slot, 1, here, :]
            p_re, p_im = probe[m, 0, here, :], probe[m, 1, here, :]
            rows_in[slot, m, r : r + STEP, :] = (p_re * o_re - p_im * o_im).astype(jnp.bfloat16)
            rows_in[slot, m, S + r : S + r + STEP, :] = (p_re * o_im + p_im * o_re).astype(jnp.bfloat16)
        half = dot(fwd[...], rows_in[slot, m])
        cols_in[m, :, 0:S] = half[0:S].astype(jnp.bfloat16)
        cols_in[m, :, S:] = half[S:].astype(jnp.bfloat16)
        wave[m] = dot(cols_in[m], bwd[...])
    alive = jnp.full((STEP, S), live[0, 0]) > slot
    for r in range(0, S, STEP):
        here = pl.ds(r, STEP)
        total = None
        for m in range(M):
            w_re, w_im = wave[m, here, 0:S], wave[m, here, S:]
            term = w_re * w_re + w_im * w_im
            total = term if m == 0 else total + term
        factor = 1.0 - counts[slot, here, :].astype(jnp.float32) / (total + background)
        factor = jnp.where(alive, factor, 0.0)
        for m in range(M):
            rows_in[slot, m, r : r + STEP, :] = (factor * wave[m, here, 0:S]).astype(jnp.bfloat16)
            rows_in[slot, m, S + r : S + r + STEP, :] = (factor * wave[m, here, S:]).astype(jnp.bfloat16)


def backward(m, probe, fwd, bwd, patch, rows_in, cols_in, wave, terms, pacc):
    for slot in range(SLOTS):
        back = dot(bwd[...], rows_in[slot, m])
        cols_in[slot, :, 0:S] = back[0:S].astype(jnp.bfloat16)
        cols_in[slot, :, S:] = back[S:].astype(jnp.bfloat16)
        wave[slot] = dot(cols_in[slot], fwd[...])
    for r in range(0, S, STEP):
        here = pl.ds(r, STEP)
        p_re, p_im = probe[m, 0, here, :], probe[m, 1, here, :]
        q_re = q_im = None
        for slot in range(SLOTS):
            c_re, c_im = wave[slot, here, 0:S], wave[slot, here, S:]
            o_re, o_im = patch[slot, 0, here, :], patch[slot, 1, here, :]
            a_re, a_im = p_re * c_re + p_im * c_im, p_re * c_im - p_im * c_re
            if m:
                a_re, a_im = terms[slot, 0, here, :] + a_re, terms[slot, 1, here, :] + a_im
            terms[slot, 0, here, :], terms[slot, 1, here, :] = a_re, a_im
            b_re, b_im = o_re * c_re + o_im * c_im, o_re * c_im - o_im * c_re
            q_re, q_im = (b_re, b_im) if slot == 0 else (q_re + b_re, q_im + b_im)
        for i in range(STEP // 8):
            g = m * PER_MODE + r // 8 + i
            pacc[g] = q_re[8 * i : 8 * i + 8]
            pacc[g + PART] = q_im[8 * i : 8 * i + 8]


def place(slot, corners, terms, spread):
    lane = lax.broadcasted_iota(jnp.int32, (8, 128), 1)
    sublane = lax.broadcasted_iota(jnp.int32, (8, 128), 0)
    nothing = jnp.zeros((8, 128), jnp.float32)
    _, _, down, over = box(corners, slot)
    ahead_by, down_by = lax.bitwise_and(over, 127), lax.bitwise_and(down, 7)
    inside = lane >= over
    for k in range(2):
        before = (nothing, nothing)
        for i in range(WROWS):
            now = (nothing, nothing)
            if i < S // 8:
                now = tuple(
                    pltpu.roll(terms[slot, k, 8 * i : 8 * i + 8, 128 * j : 128 * j + 128], down_by, 0) for j in range(2)
                )
            a, b = (pltpu.roll(jnp.where(sublane >= down, now[j], before[j]), ahead_by, 1) for j in range(2))
            before = now
            for j, v in enumerate((jnp.where(inside, a, 0.0), jnp.where(inside, b, a), jnp.where(inside, 0.0, b))):
                spread[slot, k, i + 1, j + 1] = v


def gather(corners, spread, row0, rows, cols, store):
    places = [box(corners, slot)[:2] for slot in range(SLOTS)]
    at_col = [[lax.max(lax.min(c - left0, WCOLS), -1) + 1 for c in cols] for _, left0 in places]

    def body(i, carry):
        at_row = [lax.max(lax.min(row0 // 8 + i - top0, WROWS), -1) + 1 for top0, _ in places]
        for j in range(len(cols)):
            for k in range(2):
                value = None
                for slot in range(SLOTS):
                    one = spread[slot, k, at_row[slot], at_col[slot][j]]
                    value = one if slot == 0 else value + one
                store(k, pl.multiple_of(8 * i, 8), j, value)
        return carry

    lax.fori_loop(0, rows // 8, body, 0, unroll=2)


def kernel(
    corners, live, tile, probe_hbm, photons, fwd_hbm, bwd_hbm, core_out, probe_out,
    padded, probe, counts, fwd, bwd, patch, rows_in, cols_in, wave, terms, spread, pacc,
    g_up, g_down, g_left, g_right, above, below, left_in, right_in, from_twin, acc,
    in1, in2, in3, sum1, sum2, passing, passing2, core_sum, probe_sum, send_sem, recv_sem, load_sem,
):
    r, c = lax.axis_index("rows"), lax.axis_index("cols")
    n_r, n_c = lax.axis_size("rows"), lax.axis_size("cols")
    up, down, left, right = r > 0, r < n_r - 1, c > 0, c < n_c - 1
    to_up, to_down, to_left, to_right = (r - 1, c), (r + 1, c), (r, c - 1), (r, c + 1)
    sides = ((up, to_up), (down, to_down), (left, to_left), (right, to_right))
    core = r % 2
    at = {"x": r // 16 * 2 + c // 4, "y": c % 4, "z": r // 2 % 8}
    twin = (r + 1 - 2 * core, c)

    def peer(axis, k):
        spot = dict(at)
        spot[axis] = (at[axis] + k) % AXES[axis]
        return (spot["x"] // 2 * 16 + spot["z"] * 2 + core, spot["x"] % 2 * 4 + spot["y"])

    lo, mid, hi = pl.ds(0, RIM), pl.ds(RIM, T), pl.ds(RIM + T, RIM)
    r_lo, r_mid, r_hi = pl.ds(0, RIM // 8), pl.ds(RIM // 8, T // 8), pl.ds((RIM + T) // 8, RIM // 8)
    c_lo, c_mid, c_hi = pl.ds(0, 1), pl.ds(1, T // 128), pl.ds(1 + T // 128, 1)
    loads = [
        pltpu.make_async_copy(src, dst, load_sem.at[i])
        for i, (src, dst) in enumerate(
            ((tile, padded.at[:, r_mid, c_mid]), (probe_hbm, probe), (fwd_hbm, fwd), (bwd_hbm, bwd), (photons, counts))
        )
    ]
    loads[0].start()
    n_half, middle = n_r // 2, (c == n_c // 2 - 1) | (c == n_c // 2)
    at_corner, past = (c == 0) | (c == n_c - 1), jnp.where(c < n_c // 2, n_c - 1, 0)
    back = jnp.where(c == 0, n_c // 2, n_c // 2 - 1)
    way_down = ((r == n_half - 1) & middle, (n_r - 1, past), (r == n_r - 1) & at_corner, (n_half - 1, back), (n_half, back), (r == n_half) & middle)
    way_up = ((r == n_half) & middle, (0, past), (r == 0) & at_corner, (n_half, back), (n_half - 1, back), (r == n_half - 1) & middle)
    ways = (way_down, way_up)
    peers = [twin] + [peer(axis, k) for axis in AXES for k in range(1, AXES[axis])]
    barrier = pltpu.get_barrier_semaphore()
    for there, device in sides:

        @pl.when(there)
        def _(device=device):
            pl.semaphore_signal(barrier, inc=1, device_id=device, device_id_type=MESH)

    for source, relay, is_relay, from_device, _, target in ways:

        @pl.when(is_relay)
        def _(device=from_device):
            pl.semaphore_signal(barrier, inc=1, device_id=device, device_id_type=MESH)

        @pl.when(target)
        def _(device=relay):
            pl.semaphore_signal(barrier, inc=1, device_id=device, device_id_type=MESH)

    for device in peers:
        pl.semaphore_signal(barrier, inc=1, device_id=device, device_id_type=MESH)
    for one in loads[1:]:
        one.start()
    loads[0].wait()
    pl.semaphore_wait(barrier, len(peers) + sum(jnp.where(there, 1, 0) for there, _ in sides) + sum(jnp.where(way[0], 1, 0) + jnp.where(way[2], 1, 0) for way in ways))

    count = [0]

    def copy(src, dst, device):
        index = count[0]
        count[0] += 1
        return pltpu.make_async_remote_copy(
            src_ref=src,
            dst_ref=dst,
            send_sem=send_sem.at[index],
            recv_sem=recv_sem.at[index],
            device_id=device,
            device_id_type=MESH,
        )

    sent = []

    def go(some, there=None):
        if there is None:
            for one in some:
                one.start()
        else:

            @pl.when(there)
            def _():
                for one in some:
                    one.start()

        sent.append((there, some))
        return some

    def relayed(way, pieces):
        legs = [(copy(src, buf, way[1]), copy(buf, dst, way[4])) for src, buf, dst in pieces]

        def depart(*some):
            go([legs[i][0] for i in some], way[0])

        def pass_on(*some):
            for i in some:

                @pl.when(way[2])
                def _(i=i):
                    legs[i][0].wait_recv()

                go([legs[i][1]], way[2])

        def arrive(*some):
            for i in some:
                legs[i][1].wait_recv()

        return depart, pass_on, arrive

    down_direct, up_direct = down & jnp.logical_not(way_down[0]), up & jnp.logical_not(way_up[0])
    above_direct, below_direct = up & jnp.logical_not(way_down[5]), down & jnp.logical_not(way_up[5])

    r_near, r_far = pl.ds(RIM // 8, RIM // 8), pl.ds(T // 8, RIM // 8)
    c_near, c_far = pl.ds(1, 1), pl.ds(T // 128, 1)
    spans = (r_near, r_far, pl.ds(2 * RIM // 8, (T - 2 * RIM) // 8))
    to_l = [copy(padded.at[:, s, c_near], padded.at[:, s, c_hi], to_left) for s in spans]
    to_r = [copy(padded.at[:, s, c_far], padded.at[:, s, c_lo], to_right) for s in spans]
    to_u = copy(padded.at[:, r_near, c_mid], padded.at[:, r_hi, c_mid], to_up)
    to_d = copy(padded.at[:, r_far, c_mid], padded.at[:, r_lo, c_mid], to_down)
    c_ul = copy(padded.at[:, r_near, c_lo], padded.at[:, r_hi, c_lo], to_up)
    c_ur = copy(padded.at[:, r_near, c_hi], padded.at[:, r_hi, c_hi], to_up)
    c_dl = copy(padded.at[:, r_far, c_lo], padded.at[:, r_lo, c_lo], to_down)
    c_dr = copy(padded.at[:, r_far, c_hi], padded.at[:, r_lo, c_hi], to_down)
    blocks = [pl.ds(1 + i, 1) for i in range(T // 128)] + [c_lo, c_hi]
    strips_in = range(T // 128)
    relay_down = relayed(way_down, [(padded.at[:, r_far, b], passing.at[:, :, b], padded.at[:, r_lo, b]) for b in blocks])
    relay_up = relayed(way_up, [(padded.at[:, r_near, b], passing.at[:, :, b], padded.at[:, r_hi, b]) for b in blocks])
    for i in range(3):
        go([to_l[i]], left)
        go([to_r[i]], right)
        if i == 0:
            go([to_u], up_direct)
            go([to_d], down_direct)
            relay_down[0](*strips_in)
            relay_up[0](*strips_in)

    for slot in range(SLOTS):
        spread[slot, :, 0] = jnp.zeros((2, WCOLS + 2, 8, 128), jnp.float32)
        spread[slot, :, WROWS + 1] = jnp.zeros((2, WCOLS + 2, 8, 128), jnp.float32)
        spread[slot, :, :, 0] = jnp.zeros((2, WROWS + 2, 8, 128), jnp.float32)
        spread[slot, :, :, WCOLS + 1] = jnp.zeros((2, WROWS + 2, 8, 128), jnp.float32)
    padded[:, ROWS - 1] = jnp.zeros((2, COLS, 8, 128), jnp.float32)
    padded[:, :, COLS - 1] = jnp.zeros((2, ROWS, 8, 128), jnp.float32)

    def zeroed(there, rows, cols):
        @pl.when(jnp.logical_not(there))
        def _():
            padded[:, rows, cols] = jnp.zeros((2, rows.size, cols.size, 8, 128), jnp.float32)

    def arrived(there, one, way=None, relay=None, some=()):
        @pl.when(there)
        def _():
            one.wait_recv()

        if way is not None:

            @pl.when(way[5])
            def _():
                relay[2](*some)

    for there, rows, cols in (
        (left, r_mid, c_lo), (right, r_mid, c_hi), (up, r_lo, c_mid), (down, r_hi, c_mid),
        (up & left, r_lo, c_lo), (up & right, r_lo, c_hi), (down & left, r_hi, c_lo), (down & right, r_hi, c_hi),
    ):
        zeroed(there, rows, cols)
    corner_l, corner_r = len(blocks) - 2, len(blocks) - 1
    relay_down[1](0)
    relay_up[1](0)
    arrived(left, to_r[0])
    go([c_ul], left & up_direct)
    relay_up[0](corner_l)
    arrived(right, to_l[0])
    go([c_ur], right & up_direct)
    relay_up[0](corner_r)
    relay_down[1](1)
    relay_up[1](1)
    arrived(left, to_r[1])
    go([c_dl], left & down_direct)
    relay_down[0](corner_l)
    arrived(right, to_l[1])
    go([c_dr], right & down_direct)
    relay_down[0](corner_r)
    for i in (2, 3, corner_l, corner_r):
        relay_down[1](i)
        relay_up[1](i)
    arrived(above_direct, to_d, way_down, relay_down, strips_in)
    arrived(below_direct, to_u, way_up, relay_up, strips_in)
    arrived(left, to_r[2])
    arrived(right, to_l[2])
    arrived(above_direct & left, c_dl, way_down, relay_down, (corner_l,))
    arrived(above_direct & right, c_dr, way_down, relay_down, (corner_r,))
    arrived(below_direct & left, c_ul, way_up, relay_up, (corner_l,))
    arrived(below_direct & right, c_ur, way_up, relay_up, (corner_r,))
    for one in loads[1:]:
        one.wait()

    def visit(slot, carry):
        forward(slot, corners, live, padded, probe, counts, fwd, bwd, patch, rows_in, cols_in, wave)
        return carry

    lax.fori_loop(0, SLOTS, visit, 0)

    first, other = PART * core, PART * (1 - core)
    scale = 1.0 / math.sqrt(n_r * n_c)
    flying = {}

    def sizes(m):
        a, b, d = ORDERS[m]
        return a, b, d, PART // AXES[a], PART // AXES[a] // AXES[b]

    def swap(m):
        src = pacc.at[pl.ds(m * PER_MODE + other, PART)]
        flying[m] = go([copy(src, from_twin.at[pl.ds(m * PART, PART)], twin)])

    def landed(m):
        for one in flying[m]:
            one.wait_recv()

    def reduce1(m):
        a, _, _, s, _ = sizes(m)
        landed(m)
        here = pl.ds(m * PART, PART)
        acc[here] = pacc[pl.ds(m * PER_MODE + first, PART)] + from_twin[here]
        flying[m] = go(
            [
                copy(
                    acc.at[pl.ds(m * PART + s * ((at[a] + k) % AXES[a]), s)],
                    in1.at[m, pl.ds((k - 1) * s, s)],
                    peer(a, k),
                )
                for k in range(1, AXES[a])
            ]
        )

    def reduce2(m):
        a, b, _, s, s2 = sizes(m)
        landed(m)
        total = acc[pl.ds(m * PART + s * at[a], s)]
        for k in range(AXES[a] - 1):
            total = total + in1[m, k * s : (k + 1) * s]
        sum1[m, 0:s] = total
        flying[m] = go(
            [
                copy(
                    sum1.at[m, pl.ds(s2 * ((at[b] + k) % AXES[b]), s2)],
                    in2.at[m, pl.ds((k - 1) * s2, s2)],
                    peer(b, k),
                )
                for k in range(1, AXES[b])
            ]
        )

    def reduce3(m):
        _, b, d, _, s2 = sizes(m)
        landed(m)
        total = sum1[m, pl.ds(s2 * at[b], s2)]
        for k in range(AXES[b] - 1):
            total = total + in2[m, k * s2 : (k + 1) * s2]
        sum2[m, 0:s2] = total
        mine = pl.ds(at[d] * s2, s2)
        in3[m, mine] = total
        flying[m] = go([copy(sum2.at[m, pl.ds(0, s2)], in3.at[m, mine], peer(d, k)) for k in range(1, AXES[d])])

    def gather2(m):
        a, b, d, s, s2 = sizes(m)
        landed(m)
        total = in3[m, 0:s2]
        for j in range(1, AXES[d]):
            total = total + in3[m, j * s2 : (j + 1) * s2]
        spot = pl.ds(m * PER_MODE + first + s * at[a] + s2 * at[b], s2)
        probe_sum[spot] = total * scale
        block = probe_sum.at[spot]
        flying[m] = go([copy(block, block, peer(b, k)) for k in range(1, AXES[b])])

    def gather1(m):
        a, _, _, s, _ = sizes(m)
        landed(m)
        block = probe_sum.at[pl.ds(m * PER_MODE + first + s * at[a], s)]
        flying[m] = go([copy(block, block, peer(a, k)) for k in range(1, AXES[a])])

    def gather0(m):
        landed(m)
        block = probe_sum.at[pl.ds(m * PER_MODE + first, PART)]
        flying[m] = go([copy(block, block, twin)])

    chain = (swap, reduce1, reduce2, reduce3, gather2, gather1, gather0, landed)
    done = [0] * M

    def advance(*modes):
        for m in modes:
            if done[m] < len(chain):
                chain[done[m]](m)
                done[m] += 1

    for m in range(M):
        backward(m, probe, fwd, bwd, patch, rows_in, cols_in, wave, terms, pacc)
        advance(*range(max(0, m - 1), m + 1))

    def put(slot, carry):
        place(slot, corners, terms, spread)
        return carry

    lax.fori_loop(0, SLOTS, put, 0)
    advance(3, 0)

    def into(ref):
        def store(k, row, j, value):
            ref[k, pl.ds(row, 8), 128 * j : 128 * j + 128] = value

        return store

    n_cols = E // 128
    bands = (lo, hi, mid)
    strips = [lo, hi] + [pl.ds(RIM + 128 * i, 128) for i in range(T // 128)]
    pass_down = relayed(way_down, [(g_down.at[:, :, b], passing2.at[:, :, b], above.at[:, :, b]) for b in strips])
    pass_up = relayed(way_up, [(g_up.at[:, :, b], passing2.at[:, :, b], below.at[:, :, b]) for b in strips])
    every = range(len(strips))
    gather(corners, spread, 0, RIM, range(n_cols), into(g_up))
    f_up = [copy(g_up.at[:, :, b], below.at[:, :, b], to_up) for b in bands]
    go(f_up, up_direct)
    pass_up[0](*every)
    gather(corners, spread, RIM + T, RIM, range(n_cols), into(g_down))
    f_down = [copy(g_down.at[:, :, b], above.at[:, :, b], to_down) for b in bands]
    go(f_down, down_direct)
    pass_down[0](*every)
    gather(corners, spread, RIM, T, (0,), into(g_left))
    gather(corners, spread, RIM, T, (n_cols - 1,), into(g_right))
    parts = (pl.ds(RIM, T - 2 * RIM), pl.ds(0, RIM), pl.ds(T - RIM, RIM))
    f_left = [copy(g_left.at[:, p, :], right_in.at[:, p, :], to_left) for p in parts]
    f_right = [copy(g_right.at[:, p, :], left_in.at[:, p, :], to_right) for p in parts]
    go(f_left[:1], left)
    go(f_right[:1], right)
    advance(1)
    for i in (0, 1):
        pass_down[1](i)
        pass_up[1](i)
    advance(0, 2)
    pass_down[1](2)
    pass_up[1](2)

    for i in range(2):
        arrived(above_direct, f_down[i], way_down, pass_down, (i,))

    @pl.when(up)
    def _():
        g_left[:, 0:RIM, :] += above[:, :, 0:RIM]
        g_right[:, 0:RIM, :] += above[:, :, RIM + T :]

    go(f_left[1:2], left)
    go(f_right[1:2], right)
    for i in range(2):
        arrived(below_direct, f_up[i], way_up, pass_up, (i,))

    @pl.when(down)
    def _():
        g_left[:, T - RIM :, :] += below[:, :, 0:RIM]
        g_right[:, T - RIM :, :] += below[:, :, RIM + T :]

    go(f_left[2:], left)
    go(f_right[2:], right)
    for i in every[3:]:
        pass_down[1](i)
        pass_up[1](i)
    advance(1, 3, 2)
    gather(corners, spread, RIM, T, range(1, n_cols - 1), into(core_sum))
    advance(0, 3, 1, 0, 2, 1)
    arrived(above_direct, f_down[2], way_down, pass_down, every[2:])

    @pl.when(up)
    def _():
        core_sum[:, 0:RIM, :] += above[:, :, RIM : RIM + T]

    arrived(below_direct, f_up[2], way_up, pass_up, every[2:])

    @pl.when(down)
    def _():
        core_sum[:, T - RIM :, :] += below[:, :, RIM : RIM + T]

    advance(3, 2, 0, 3, 1)

    @pl.when(left)
    def _():
        for one in f_right:
            one.wait_recv()
        core_sum[:, :, 0:RIM] += left_in[...]

    @pl.when(right)
    def _():
        for one in f_left:
            one.wait_recv()
        core_sum[:, :, T - RIM :] += right_in[...]

    stores = [pltpu.make_async_copy(core_sum, core_out, load_sem.at[0])]
    stores[0].start()
    advance(2, 3)
    for m in range(M):
        advance(m)
        whole = pl.ds(m * PER_MODE, PER_MODE)
        stores.append(pltpu.make_async_copy(probe_sum.at[whole], probe_out.at[whole], load_sem.at[m + 1]))
        stores[-1].start()
    for one in stores:
        one.wait()
    for there, some in sent:
        if there is None:
            for one in some:
                one.wait_send()
        else:

            @pl.when(there)
            def _(some=some):
                for one in some:
                    one.wait_send()


def on_device(object_field, probe, photons, positions, live_counts):
    fwd = dft_table(S)
    f32, bf16 = jnp.float32, jnp.bfloat16
    tile = object_field.reshape(2, T // 8, 8, T // 128, 128).transpose(0, 1, 3, 2, 4)
    smem, anywhere = (pl.BlockSpec(memory_space=m) for m in (pltpu.SMEM, pl.ANY))
    core, probe_grad = pl.pallas_call(
        kernel,
        out_shape=(
            jax.ShapeDtypeStruct((2, T, T), f32),
            jax.ShapeDtypeStruct((GROUPS, 8, S), f32),
        ),
        in_specs=[smem, smem, anywhere, anywhere, anywhere, anywhere, anywhere],
        out_specs=(anywhere, anywhere),
        scratch_shapes=[
            pltpu.VMEM((2, ROWS, COLS, 8, 128), f32),
            pltpu.VMEM((M, 2, S, S), f32),
            pltpu.VMEM((SLOTS, S, S), jnp.int32),
            pltpu.VMEM((2 * S, 2 * S), bf16),
            pltpu.VMEM((2 * S, 2 * S), bf16),
            pltpu.VMEM((SLOTS, 2, S, S), f32),
            pltpu.VMEM((SLOTS, M, 2 * S, S), bf16),
            pltpu.VMEM((M, S, 2 * S), bf16),
            pltpu.VMEM((M, S, 2 * S), f32),
            pltpu.VMEM((SLOTS, 2, S, S), f32),
            pltpu.VMEM((SLOTS, 2, WROWS + 2, WCOLS + 2, 8, 128), f32),
            pltpu.VMEM((GROUPS, 8, S), f32),
            pltpu.VMEM((2, RIM, E), f32),
            pltpu.VMEM((2, RIM, E), f32),
            pltpu.VMEM((2, T, RIM), f32),
            pltpu.VMEM((2, T, RIM), f32),
            pltpu.VMEM((2, RIM, E), f32),
            pltpu.VMEM((2, RIM, E), f32),
            pltpu.VMEM((2, T, RIM), f32),
            pltpu.VMEM((2, T, RIM), f32),
            pltpu.VMEM((GROUPS // 2, 8, S), f32),
            pltpu.VMEM((GROUPS // 2, 8, S), f32),
            pltpu.VMEM((M, PART, 8, S), f32),
            pltpu.VMEM((M, PART // 4, 8, S), f32),
            pltpu.VMEM((M, PART // 2, 8, S), f32),
            pltpu.VMEM((M, PART // 4, 8, S), f32),
            pltpu.VMEM((M, PART // 16, 8, S), f32),
            pltpu.VMEM((2, RIM // 8, E // 128, 8, 128), f32),
            pltpu.VMEM((2, RIM, E), f32),
            pltpu.VMEM((2, T, T), f32),
            pltpu.VMEM((GROUPS, 8, S), f32),
            pltpu.SemaphoreType.DMA((N_COPIES,)),
            pltpu.SemaphoreType.DMA((N_COPIES,)),
            pltpu.SemaphoreType.DMA((5,)),
        ],
        compiler_params=pltpu.CompilerParams(collective_id=0, has_side_effects=True, vmem_limit_bytes=60 << 20),
    )(positions[0, 0].T, live_counts, tile, probe, photons[0, 0], fwd, fwd.T.copy())
    return core, probe_grad.reshape(M, 2, S, S)


def solution(mesh):
    in_specs = (
        P(None, "rows", "cols"),
        P(),
        P("rows", "cols", None, None, None),
        P("rows", "cols", None, None),
        P("rows", "cols"),
    )
    out_specs = (P(None, "rows", "cols"), P())
    return jax.shard_map(on_device, mesh=mesh, in_specs=in_specs, out_specs=out_specs, check_vma=False)
```

time: 505 us -> 93.8 us (0.19)
  waiting for transfers between devices: 274 us -> 0 us
  Pallas kernels: 0 us -> 87.8 us
  matrix products: 83.6 us -> 0 us
  local copies, waits for them, and re-layouts: 52.9 us -> 4.55 us
  other arithmetic: 31.6 us -> 0 us
  starting transfers between devices: 27.7 us -> 0 us
  loops' own time: 18.2 us -> 0 us
  between operations: 14.3 us -> 1.29 us
    psum x1 -> x0, waiting for transfers between devices: 250 us -> none  [on_device(): probe_total = lax.psum(probe_acc, ('rows', 'cols'))]
    pallas_call x0 -> x1, Pallas kernels: none -> 87.8 us  [on_device(): pl.pallas_call(kernel, out_shape=(jax.ShapeDtypeStruct((2, T, T), f32), j...]
    dot_general x64 -> x0, matrix products: 83.6 us -> none  [the longest x32 43.1 us: batch_right(): jnp.einsum('mab,bc->mac', values, table, preferred_element_type=jnp.float32)]
    ppermute x8 -> x0, starting transfers between devices: 27.6 us -> none  [the longest x4 16.3 us: shifted(): lax.ppermute(value, axis, [(source, source + steps) for source in range(l...]
    dynamic_update_slice x4 -> x0, local copies, waits for them, and re-layouts: 25.8 us -> none  [visit(): lax.dynamic_update_slice(gradient, before + object_term, (anchor, top_row...]
    ppermute x8 -> x0, waiting for transfers between devices: 23.7 us -> none  [the longest x2 12.3 us: extended(): lax.ppermute(tail, axis, [(i, (i + 1) % count) for i in range(ends)])]
    another operation x1 -> x0, loops' own time: 18.2 us -> none  [on_device(): lax.fori_loop(0, slot_total, lambda slot_id, state: visit(slot_id, state)...]
    add x9 -> x0, other arithmetic: 17 us -> none  [the longest x4 11.4 us: visit(): return (gradient, probe_acc + probe_term)]
  transfers between devices with their start and end apart: 9 -> 0, of which waited for: 6 -> 0; matrix products, arithmetic and copies ran while one was open for 3% -> 0% of each run, Pallas kernels for 0% -> 0%
where the time goes in v2:
time: 93.8 us; the launch traced here: 93.7 us
  Pallas kernels  87.8 us (94%)
  local copies, waits for them, and re-layouts  4.55 us (5%)
  between operations  1.29 us (1%)
    pallas_call x1, Pallas kernels, on_device(): pl.pallas_call(kernel, out_shape=(jax.ShapeDtypeStruct((2, T, T), f32), j...  87.8 us
    unnamed x4, local copies, waits for them, and re-layouts  4.55 us

profile of v2, /device:TPU:1, one launch (start us, length us, event | category | flops | bytes accessed | tf_op | source)
XLA Modules:
  0.0 93.7 jit_solution(14168684032022724390)
XLA Ops:
  1.3 87.8 %shard_map.86 = (f32[2,512,512]{2,1,0:T(8,128)}, f32[256,8,256]{2,1,0:T(8,128)}) custom-call(s32[2,4]{1,0:T(2,128)} %bitcast.11, s32[1,1]{1,0:T(1,128)S(6)} %copy.11.live, f32[2,64,4,8,128]{4,3,2,1,0:T(8,128)} %bitcast.8, f32[4,2,256,256]{3,2,1,0:T(8,128)} %probe_hbm.1, s32[4,256,256]{2,1,0:T(8,128)} %bitcast.10, bf16[512,512]{1,0:T(8,128)(2,1)} %constant.4.clone.fwd_hbm, ...), custom_call_target="tpu_custom_call" | custom-call | tf_op jit(solution)/shard_map/pallas_call | solution.py:580
  89.1 0.0 copy-start
  89.1 3.2 %copy.12 = f32[2,512,512]{2,1,0:T(8,128)} copy(f32[2,512,512]{2,1,0:T(8,128)} %get-tuple-element.8) | data formatting | bytes 4194304
  92.4 0.0 copy-done
  92.4 1.3 %copy.13 = f32[4,2,256,256]{3,2,1,0:T(8,128)} copy(f32[4,2,256,256]{3,2,1,0:T(8,128)S(1)} %bitcast.9) | data formatting | bytes 4194304
Async XLA Ops:
  89.1 3.2 %copy-start = (f32[256,8,256]{2,1,0:T(8,128)S(1)}, f32[256,8,256]{2,1,0:T(8,128)}, u32[]{:S(2)}) copy-start(f32[256,8,256]{2,1,0:T(8,128)} %get-tuple-element.5) | copy-start | bytes 6291460

commit v3 on v2

--- a/solution.py
+++ b/solution.py
@@ -156,7 +156,7 @@
 
 
 def kernel(
-    corners, live, tile, probe_hbm, photons, fwd_hbm, bwd_hbm, core_out, probe_out,
+    corners, live, tile, probe_hbm, photons, fwd_hbm, bwd_hbm, core_out, left_out, right_out, probe_out,
     padded, probe, counts, fwd, bwd, patch, rows_in, cols_in, wave, terms, spread, pacc,
     g_up, g_down, g_left, g_right, above, below, left_in, right_in, from_twin, acc,
     in1, in2, in3, sum1, sum2, passing, passing2, core_sum, probe_sum, send_sem, recv_sem, load_sem,
@@ -324,23 +324,21 @@
     ):
         zeroed(there, rows, cols)
     corner_l, corner_r = len(blocks) - 2, len(blocks) - 1
-    relay_down[1](0)
-    relay_up[1](0)
+    relay_down[1](*strips_in)
+    relay_up[1](*strips_in)
     arrived(left, to_r[0])
     go([c_ul], left & up_direct)
     relay_up[0](corner_l)
     arrived(right, to_l[0])
     go([c_ur], right & up_direct)
     relay_up[0](corner_r)
-    relay_down[1](1)
-    relay_up[1](1)
     arrived(left, to_r[1])
     go([c_dl], left & down_direct)
     relay_down[0](corner_l)
     arrived(right, to_l[1])
     go([c_dr], right & down_direct)
     relay_down[0](corner_r)
-    for i in (2, 3, corner_l, corner_r):
+    for i in (corner_l, corner_r):
         relay_down[1](i)
         relay_up[1](i)
     arrived(above_direct, to_d, way_down, relay_down, strips_in)
@@ -361,7 +359,6 @@
     lax.fori_loop(0, SLOTS, visit, 0)
 
     first, other = PART * core, PART * (1 - core)
-    scale = 1.0 / math.sqrt(n_r * n_c)
     flying = {}
 
     def sizes(m):
@@ -428,7 +425,7 @@
         for j in range(1, AXES[d]):
             total = total + in3[m, j * s2 : (j + 1) * s2]
         spot = pl.ds(m * PER_MODE + first + s * at[a] + s2 * at[b], s2)
-        probe_sum[spot] = total * scale
+        probe_sum[spot] = total
         block = probe_sum.at[spot]
         flying[m] = go([copy(block, block, peer(b, k)) for k in range(1, AXES[b])])
 
@@ -460,8 +457,10 @@
         place(slot, corners, terms, spread)
         return carry
 
-    lax.fori_loop(0, SLOTS, put, 0)
-    advance(3, 0)
+    lax.fori_loop(0, SLOTS // 2, put, 0)
+    advance(3)
+    lax.fori_loop(SLOTS // 2, SLOTS, put, 0)
+    advance(0)
 
     def into(ref):
         def store(k, row, j, value):
@@ -490,13 +489,10 @@
     f_right = [copy(g_right.at[:, p, :], left_in.at[:, p, :], to_right) for p in parts]
     go(f_left[:1], left)
     go(f_right[:1], right)
-    advance(1)
+    advance(1, 0, 2, 3)
     for i in (0, 1):
         pass_down[1](i)
         pass_up[1](i)
-    advance(0, 2)
-    pass_down[1](2)
-    pass_up[1](2)
 
     for i in range(2):
         arrived(above_direct, f_down[i], way_down, pass_down, (i,))
@@ -518,12 +514,13 @@
 
     go(f_left[2:], left)
     go(f_right[2:], right)
-    for i in every[3:]:
+    advance(1, 2)
+    for i in every[2:]:
         pass_down[1](i)
         pass_up[1](i)
-    advance(1, 3, 2)
+    advance(3)
     gather(corners, spread, RIM, T, range(1, n_cols - 1), into(core_sum))
-    advance(0, 3, 1, 0, 2, 1)
+    advance(0, 1, 2, 3, 0, 1, 2)
     arrived(above_direct, f_down[2], way_down, pass_down, every[2:])
 
     @pl.when(up)
@@ -536,30 +533,31 @@
     def _():
         core_sum[:, T - RIM :, :] += below[:, :, RIM : RIM + T]
 
-    advance(3, 2, 0, 3, 1)
-
-    @pl.when(left)
-    def _():
-        for one in f_right:
-            one.wait_recv()
-        core_sum[:, :, 0:RIM] += left_in[...]
-
-    @pl.when(right)
-    def _():
-        for one in f_left:
-            one.wait_recv()
-        core_sum[:, :, T - RIM :] += right_in[...]
-
     stores = [pltpu.make_async_copy(core_sum, core_out, load_sem.at[0])]
     stores[0].start()
-    advance(2, 3)
+    advance(3, 0, 1, 2)
+    for there, some, ref, out in ((left, f_right, left_in, left_out), (right, f_left, right_in, right_out)):
+
+        @pl.when(there)
+        def _(some=some):
+            for one in some:
+                one.wait_recv()
+
+        @pl.when(jnp.logical_not(there))
+        def _(ref=ref):
+            ref[...] = jnp.zeros_like(ref)
+
+        stores.append(pltpu.make_async_copy(ref, out, load_sem.at[len(stores)]))
+        stores[-1].start()
+    advance(3)
     for m in range(M):
         advance(m)
         whole = pl.ds(m * PER_MODE, PER_MODE)
-        stores.append(pltpu.make_async_copy(probe_sum.at[whole], probe_out.at[whole], load_sem.at[m + 1]))
+        stores.append(pltpu.make_async_copy(probe_sum.at[whole], probe_out.at[whole], load_sem.at[len(stores)]))
         stores[-1].start()
     for one in stores:
         one.wait()
+
     for there, some in sent:
         if there is None:
             for one in some:
@@ -577,14 +575,16 @@
     f32, bf16 = jnp.float32, jnp.bfloat16
     tile = object_field.reshape(2, T // 8, 8, T // 128, 128).transpose(0, 1, 3, 2, 4)
     smem, anywhere = (pl.BlockSpec(memory_space=m) for m in (pltpu.SMEM, pl.ANY))
-    core, probe_grad = pl.pallas_call(
+    core, left, right, probe_total = pl.pallas_call(
         kernel,
         out_shape=(
             jax.ShapeDtypeStruct((2, T, T), f32),
+            jax.ShapeDtypeStruct((2, T, RIM), f32),
+            jax.ShapeDtypeStruct((2, T, RIM), f32),
             jax.ShapeDtypeStruct((GROUPS, 8, S), f32),
         ),
         in_specs=[smem, smem, anywhere, anywhere, anywhere, anywhere, anywhere],
-        out_specs=(anywhere, anywhere),
+        out_specs=(anywhere,) * 4,
         scratch_shapes=[
             pltpu.VMEM((2, ROWS, COLS, 8, 128), f32),
             pltpu.VMEM((M, 2, S, S), f32),
@@ -619,11 +619,14 @@
             pltpu.VMEM((GROUPS, 8, S), f32),
             pltpu.SemaphoreType.DMA((N_COPIES,)),
             pltpu.SemaphoreType.DMA((N_COPIES,)),
-            pltpu.SemaphoreType.DMA((5,)),
+            pltpu.SemaphoreType.DMA((3 + M,)),
         ],
         compiler_params=pltpu.CompilerParams(collective_id=0, has_side_effects=True, vmem_limit_bytes=60 << 20),
     )(positions[0, 0].T, live_counts, tile, probe, photons[0, 0], fwd, fwd.T.copy())
-    return core, probe_grad.reshape(M, 2, S, S)
+    keep = ((0, 0), (0, 0))
+    object_grad = core + jnp.pad(left, (*keep, (0, T - RIM))) + jnp.pad(right, (*keep, (T - RIM, 0)))
+    probe_grad = probe_total.reshape(M, 2, S, S) / math.sqrt(lax.axis_size("rows") * lax.axis_size("cols"))
+    return object_grad, probe_grad
 
 
 def solution(mesh):

time: 93.8 us -> 89.5 us (0.954)
  other arithmetic: 0 us -> 5 us
  Pallas kernels: 87.8 us -> 83.1 us
  local copies, waits for them, and re-layouts: 4.55 us -> 0.01 us
    pallas_call x1, Pallas kernels: 87.8 us -> 83.1 us  [on_device(): pl.pallas_call(kernel, out_shape=(jax.ShapeDtypeStruct((2, T, T), f32), j...]
    unnamed x4 -> x2, local copies, waits for them, and re-layouts: 4.55 us -> 0.01 us
    add x0 -> x1, other arithmetic: none -> 3.54 us  [on_device(): core + jnp.pad(left, (*keep, (0, T - RIM)))]
    div x0 -> x1, other arithmetic: none -> 1.46 us  [on_device(): probe_total.reshape(M, 2, S, S)]
where the time goes in v3:
time: 89.5 us; the launch traced here: 89.4 us
  Pallas kernels  83.1 us (93%)
  other arithmetic  5 us (6%)
  between operations  1.29 us (1%)
    pallas_call x1, Pallas kernels, on_device(): pl.pallas_call(kernel, out_shape=(jax.ShapeDtypeStruct((2, T, T), f32), j...  83.1 us
    add x1, other arithmetic, on_device(): core + jnp.pad(left, (*keep, (0, T - RIM)))  3.54 us

profile of v3, /device:TPU:1, one launch (start us, length us, event | category | flops | bytes accessed | tf_op | source)
XLA Modules:
  0.0 89.4 jit_solution(1072543306074531649)
XLA Ops:
  1.3 83.1 %shard_map.86 = (f32[2,512,512]{2,1,0:T(8,128)}, f32[2,512,128]{2,1,0:T(8,128)}, f32[2,512,128]{2,1,0:T(8,128)}, f32[256,8,256]{2,1,0:T(8,128)}) custom-call(s32[2,4]{1,0:T(2,128)} %bitcast.11, s32[1,1]{1,0:T(1,128)S(6)} %copy.9.live, f32[2,64,4,8,128]{4,3,2,1,0:T(8,128)} %bitcast.8, f32[4,2,256,256]{3,2,1,0:T(8,128)} %probe_hbm.1, s32[4,256,256]{2,1,0:T(8,128)} %bitcast.10, ...), custom_call_target="tpu_custom_call" | custom-call | tf_op jit(solution)/shard_map/pallas_call | solution.py:578
  84.4 0.0 copy-start
  84.4 3.5 %pad_add_fusion = f32[2,512,512]{2,1,0:T(8,128)} fusion(f32[2,512,128]{2,1,0:T(8,128)} %get-tuple-element.8, f32[2,512,512]{2,1,0:T(8,128)} %get-tuple-element.6, f32[2,512,128]{2,1,0:T(8,128)} %get-tuple-element.7), kind=kLoop, calls=%fused_computation | loop fusion | flops 1048576 | bytes 5242880 | tf_op jit(solution)/shard_map/add | solution.py:627
  87.9 0.0 copy-done
  87.9 1.5 %broadcast_multiply_fusion = f32[256,8,256]{2,1,0:T(8,128)} fusion(f32[256,8,256]{2,1,0:T(8,128)S(1)} %copy-done), kind=kLoop, calls=%fused_computation.1 | loop fusion | flops 524288 | bytes 4194304 | tf_op jit(solution)/shard_map/div | solution.py:628
Async XLA Ops:
  84.4 3.6 %copy-start = (f32[256,8,256]{2,1,0:T(8,128)S(1)}, f32[256,8,256]{2,1,0:T(8,128)}, u32[]{:S(2)}) copy-start(f32[256,8,256]{2,1,0:T(8,128)} %get-tuple-element.9) | copy-start | bytes 6291460

commit v4 on v3

--- a/solution.py
+++ b/solution.py
@@ -623,8 +623,9 @@
         ],
         compiler_params=pltpu.CompilerParams(collective_id=0, has_side_effects=True, vmem_limit_bytes=60 << 20),
     )(positions[0, 0].T, live_counts, tile, probe, photons[0, 0], fwd, fwd.T.copy())
-    keep = ((0, 0), (0, 0))
-    object_grad = core + jnp.pad(left, (*keep, (0, T - RIM))) + jnp.pad(right, (*keep, (T - RIM, 0)))
+    object_grad = jnp.concatenate(
+        [core[:, :, :RIM] + left, core[:, :, RIM : T - RIM], core[:, :, T - RIM :] + right], axis=2
+    )
     probe_grad = probe_total.reshape(M, 2, S, S) / math.sqrt(lax.axis_size("rows") * lax.axis_size("cols"))
     return object_grad, probe_grad
 

time: 89.5 us -> 90.4 us (1.010)
  local copies, waits for them, and re-layouts: 0.01 us -> 1.32 us
    add x1, other arithmetic: 3.54 us -> 1.79 us  [on_device(): core[:, :, :RIM] + left]
    concatenate x0 -> x1, other arithmetic: none -> 1.57 us  [on_device(): jnp.concatenate([core[:, :, :RIM] + left, core[:, :, RIM:T - RIM], core[:...]
    unnamed x2 -> x4, local copies, waits for them, and re-layouts: 0.01 us -> 1.22 us
where the time goes in v4:
time: 90.4 us
  Pallas kernels  83 us (92%)
  other arithmetic  4.81 us (5%)
  local copies, waits for them, and re-layouts  1.32 us (1%)
  between operations  1.31 us (1%)
    pallas_call x1, Pallas kernels, on_device(): pl.pallas_call(kernel, out_shape=(jax.ShapeDtypeStruct((2, T, T), f32), j...  83 us

profile of v4, /device:TPU:1, one launch (start us, length us, event | category | flops | bytes accessed | tf_op | source)
XLA Modules:
  0.0 90.4 jit_solution(550680025319699470)
XLA Ops:
  1.3 83.0 %shard_map.86 = (f32[2,512,512]{2,1,0:T(8,128)}, f32[2,512,128]{2,1,0:T(8,128)}, f32[2,512,128]{2,1,0:T(8,128)}, f32[256,8,256]{2,1,0:T(8,128)}) custom-call(s32[2,4]{1,0:T(2,128)} %bitcast.11, s32[1,1]{1,0:T(1,128)S(6)} %copy.9.live, f32[2,64,4,8,128]{4,3,2,1,0:T(8,128)} %bitcast.8, f32[4,2,256,256]{3,2,1,0:T(8,128)} %probe_hbm.1, s32[4,256,256]{2,1,0:T(8,128)} %bitcast.10, ...), custom_call_target="tpu_custom_call" | custom-call | tf_op jit(solution)/shard_map/pallas_call | solution.py:578
  84.3 0.0 copy-start
  84.3 1.8 %slice_add_fusion.1 = (f32[2,512,128]{2,1,0:T(8,128)S(1)}, f32[2,512,128]{2,1,0:T(8,128)S(1)}) fusion(f32[2,512,128]{2,1,0:T(8,128)} %get-tuple-element.7, f32[2,512,512]{2,1,0:T(8,128)} %get-tuple-element.6, f32[2,512,128]{2,1,0:T(8,128)} %get-tuple-element.8), kind=kLoop, calls=%fused_computation.3 | loop fusion | flops 262144 | bytes 3145728 | tf_op jit(solution)/shard_map/add | solution.py:627
  86.1 0.4 copy-done
  86.5 0.1 slice.10
  86.6 0.0 copy-start.1
  86.6 1.6 %pad_maximum_fusion = f32[2,512,512]{2,1,0:T(8,128)} fusion(f32[2,512,128]{2,1,0:T(8,128)S(1)} %get-tuple-element.11, f32[2,512,256]{2,1,0:T(8,128)S(1)} %slice.10, f32[2,512,128]{2,1,0:T(8,128)S(1)} %get-tuple-element.10), kind=kLoop, calls=%fused_computation | loop fusion | flops 1048576 | bytes 4194304 | tf_op jit(solution)/shard_map/concatenate | solution.py:626
  88.2 0.8 copy-done.1
  89.0 1.5 %broadcast_multiply_fusion = f32[256,8,256]{2,1,0:T(8,128)} fusion(f32[256,8,256]{2,1,0:T(8,128)S(1)} %copy-done.1), kind=kLoop, calls=%fused_computation.1 | loop fusion | flops 524288 | bytes 4194304 | tf_op jit(solution)/shard_map/div | solution.py:629
Async XLA Ops:
  84.3 2.2 %copy-start = (f32[2,512,512]{2,1,0:T(8,128)S(1)}, f32[2,512,512]{2,1,0:T(8,128)}, u32[]{:S(2)}) copy-start(f32[2,512,512]{2,1,0:T(8,128)} %get-tuple-element.6) | copy-start | bytes 6291460
  86.6 2.3 %copy-start.1 = (f32[256,8,256]{2,1,0:T(8,128)S(1)}, f32[256,8,256]{2,1,0:T(8,128)}, u32[]{:S(2)}) copy-start(f32[256,8,256]{2,1,0:T(8,128)} %get-tuple-element.9) | copy-start | bytes 6291460
